TPU v7x, 128 devices: a whole 4x4x4 slice. The times are simulated.
128 devices in a mesh: owner: 32 (over y, z, core), task: 4 (over x).
Axes of the slice: x: 4, y: 4, z: 4, core: 2. Of those that a mesh axis runs over, the one named last changes fastest.
Arguments:
- amplitudes: bfloat16 [768, 20, 32, 256], P('owner'), may hold values from -6 to 6
- integrals: bfloat16 [20, 32, 8192, 256], P(None, 'owner', 'task'), may hold values from -0.015625 to 0.015625
- nonzero_tiles: int32 [32, 18], replicated, may hold values from 0 to 19, as said below
Outputs:
- ladder: float32 [768, 8192], P('owner', 'task')
Inputs may be any that keep to these rules, and one draw needn't show every extreme that they name: `nonzero_tiles`: each row o holds 18 different tile slots of owner o; tiles not listed do not enter.
All inputs are finite; a program needn't handle non-finite values.
Results may differ from a plain program's by a relative error of at most 0.0003.
Values may be sent and summed in bfloat16 or wider, within the bound.
No kernel may reach another device: no remote copies, remote signals or barrier semaphores. Data moves between devices by JAX's collectives and lax.ppermute only.
A program may use at most 128 MiB of HBM per device.

v0:
```python
import jax
import jax.numpy as jnp
from jax import lax
from jax.sharding import PartitionSpec as P


def per_device(amplitudes, integrals, nonzero_tiles):
    owner_index = lax.axis_index("owner")
    mine = lax.dynamic_index_in_dim(nonzero_tiles, owner_index, 0, False)
    flat = lax.all_to_all(amplitudes, "owner", split_axis=2, concat_axis=0, tiled=True)[:, :, 0, :]
    received = jnp.take(flat, mine, axis=1)
    int_live = jnp.take(integrals[:, 0], mine, axis=0)
    return lax.psum_scatter(
        jnp.einsum("plx,lax->pa", received, int_live, preferred_element_type=jnp.float32),
        "owner",
        scatter_dimension=0,
        tiled=True,
    )


def solution(mesh):
    placed = (P("owner", None, None, None), P(None, "owner", "task", None), P())
    return jax.shard_map(
        per_device, mesh=mesh, in_specs=placed, out_specs=P("owner", "task"), check_vma=False
    )
```

profile of v0, /device:TPU:0, one launch (start us, length us, event | category | flops | bytes accessed | tf_op | source)
XLA Modules:
  0.0 274.6 jit_solution(13212143237377941908)
XLA Ops:
  6.5 0.0 copy-start
  6.5 10.8 %copy.5 = bf16[24,20,32,256]{3,0,1,2:T(8,128)(2,1)} copy(bf16[24,20,32,256]{3,2,1,0:T(8,128)(2,1)} %param.3) | data formatting | bytes 15728640 | tf_op args[0]
  17.3 8.5 %all-to-all-start = ((bf16[24,20,32,256]{3,0,1,2:T(8,128)(2,1)}), bf16[24,20,32,256]{3,0,1,2:T(8,128)(2,1)}, u32[]{:S(2)}, u32[]{:S(2)}) async-start(bf16[24,20,32,256]{3,0,1,2:T(8,128)(2,1)} %copy.5), calls=%async_computation | async-start | bytes 15728640 | tf_op jit(solution)/shard_map/all_to_all | solution.py:10
  25.9 0.0 reduce-scatter.2.cloned.1.call-start
  25.9 0.0 copy-done
  26.0 0.2 dynamic-slice_reduce_fusion
  26.2 15.1 %gather_fusion.1 = bf16[18,2048,256]{2,1,0:T(8,128)(2,1)} fusion(bf16[20,2048,256]{2,1,0:T(8,128)(2,1)} %bitcast.18, s32[1024]{0:T(1024)S(1)} %pad_clamp_fusion), kind=kCustom, calls=%fused_computation.1 | custom fusion | bytes 37748808 | tf_op jit(solution)/shard_map/jit(_take)/gather | solution.py:12
  41.2 91.0 %all-to-all-done = bf16[24,20,32,256]{3,0,1,2:T(8,128)(2,1)} async-done(((bf16[24,20,32,256]{3,0,1,2:T(8,128)(2,1)}), bf16[24,20,32,256]{3,0,1,2:T(8,128)(2,1)}, u32[]{:S(2)}, u32[]{:S(2)}) %all-to-all-start) | async-done | bytes 7864352 | tf_op jit(solution)/shard_map/all_to_all | solution.py:10
  132.3 7.2 %copy.6 = bf16[24,20,32,256]{3,0,2,1:T(8,128)(2,1)} copy(bf16[24,20,32,256]{3,0,1,2:T(8,128)(2,1)} %all-to-all-done) | data formatting | bytes 15728640 | tf_op jit(solution)/shard_map/all_to_all | solution.py:10
  139.5 8.3 %gather_fusion = bf16[18,768,256]{2,1,0:T(8,128)(2,1)} fusion(bf16[768,20,256]{2,0,1:T(8,128)(2,1)} %bitcast.17, s32[1024]{0:T(1024)S(1)} %pad_clamp_fusion), kind=kCustom, calls=%fused_computation | custom fusion | bytes 14155848 | tf_op jit(solution)/shard_map/jit(_take)/gather | solution.py:11
  147.8 0.0 copy-start.1
  147.8 21.4 %fusion.7 = f32[768,2048]{1,0:T(8,128)} fusion(bf16[18,2048,256]{2,1,0:T(8,128)(2,1)} %gather_fusion.1, pred[18]{0:T(512)(128)(4,1)S(1)} %compare_and_fusion, bf16[18,768,256]{2,1,0:T(8,128)(2,1)} %gather_fusion), kind=kOutput, calls=%fused_computation.9 | convolution fusion | flops 14508490752 | bytes 32243730 | tf_op jit(solution)/shard_map/plx,lax->pa/dot_general | solution.py:14
  169.2 0.0 reduce-scatter.2.cloned.1.call-update
  169.2 98.5 %reduce-scatter.2.cloned.1.call-done = f32[24,2048]{1,0:T(8,128)} async-done(((f32[768,2048]{1,0:T(8,128)}), f32[24,2048]{1,0:T(8,128)}) %reduce-scatter.2.cloned.1.call-update) | async-done | bytes 196624 | tf_op jit(solution)/shard_map/reduce_scatter | solution.py:13
  267.7 0.0 copy-done.1
  (3 shorter events, 0.0 us)
Async XLA Ops:
  6.5 19.4 %copy-start = (s32[32,18]{0,1:T(8,128)S(1)}, s32[32,18]{0,1:T(8,128)}, u32[]{:S(2)}) copy-start(s32[32,18]{0,1:T(8,128)} %param.5) | copy-start | bytes 6916
  17.3 114.9 %all-to-all-start = ((bf16[24,20,32,256]{3,0,1,2:T(8,128)(2,1)}), bf16[24,20,32,256]{3,0,1,2:T(8,128)(2,1)}, u32[]{:S(2)}, u32[]{:S(2)}) async-start(bf16[24,20,32,256]{3,0,1,2:T(8,128)(2,1)} %copy.5), calls=%async_computation | async-start | bytes 15728640 | tf_op jit(solution)/shard_map/all_to_all | solution.py:10
  25.9 241.8 %reduce-scatter.2.cloned.1.call-start = ((), (), s32[]{:S(2)}) async-start(), calls=%async_computation.2 | async-start | bytes 6488064 | tf_op jit(solution)/shard_map/reduce_scatter | solution.py:13
  147.8 119.9 %copy-start.1 = (s32[32,18]{0,1:T(8,128)S(1)}, s32[32,18]{0,1:T(8,128)}, u32[]{:S(2)}) copy-start(s32[32,18]{0,1:T(8,128)} %param.5) | copy-start | bytes 6916
Sparse Core Ops, SparseCore 0:
  169.3 98.3 reduce-scatter.1
where the time goes:
time: 275 us
  waiting for transfers between devices  190 us (69%)
  local copies, waits for them, and re-layouts  41.6 us (15%)
  matrix products  21.4 us (8%)
  between operations  13.4 us (5%)
  starting transfers between devices  8.57 us (3%)
    reduce_scatter x1, waiting for transfers between devices, per_device(): lax.psum_scatter(jnp.einsum('plx,lax->pa', received, int_live, preferred_...  98.5 us
    all_to_all x1, waiting for transfers between devices, per_device(): lax.all_to_all(amplitudes, 'owner', split_axis=2, concat_axis=0, tiled=True)  91 us
    dot_general x1, matrix products, per_device(): jnp.einsum('plx,lax->pa', received, int_live, preferred_element_type=jnp....  21.4 us
    gather x1, local copies, waits for them, and re-layouts, per_device(): int_live = jnp.take(integrals[:, 0], mine, axis=0)  15.1 us
    unnamed x5, local copies, waits for them, and re-layouts  10.8 us
    all_to_all x1, starting transfers between devices, per_device(): lax.all_to_all(amplitudes, 'owner', split_axis=2, concat_axis=0, tiled=True)  8.53 us
    gather x1, local copies, waits for them, and re-layouts, per_device(): received = jnp.take(flat, mine, axis=1)  8.35 us
    all_to_all x1, local copies, waits for them, and re-layouts, per_device(): lax.all_to_all(amplitudes, 'owner', split_axis=2, concat_axis=0, tiled=True)  7.19 us
  transfers between devices with their start and end apart: 2, of which 2 were waited for; matrix products, arithmetic and copies ran while one was open for 6% of the time, Pallas kernels for 0%

commit v1 on v0

v1 whole, which is shorter than its diff:
```python
import functools

import jax
import jax.numpy as jnp
from jax import lax
from jax.experimental import pallas as pl
from jax.experimental.pallas import tpu as pltpu
from jax.sharding import PartitionSpec as P

OWNERS, TASKS, SIDE = 32, 4, 4
QUARTER = 2
SHARED = QUARTER * TASKS
BUNDLE = 5
GROUP = 8
F32 = jnp.float32


def owner_at(y, z, c):
    return ((y % SIDE) * SIDE + z % SIDE) * 2 + c


def owner_perm(move):
    return [
        (owner_at(y, z, c), owner_at(*move(y, z, c)))
        for y in range(SIDE)
        for z in range(SIDE)
        for c in range(2)
    ]


def along(step, cores_swapped):
    return owner_perm(
        lambda y, z, c: (y, z + step, c) if c == cores_swapped else (y + step, z, c)
    )


def shift_task(step):
    return [(t, (t + step) % TASKS) for t in range(TASKS)]


def pack_kernel(by_task, first, nz_ref, amp_ref, out_ref, listed, source, nz_sem, sem):
    owners, count, pairs, ct = out_ref.shape
    tiles = source.shape[0]
    start = first + (lax.axis_index("task") * count if by_task else 0)
    copies = [pltpu.make_async_copy(nz_ref, listed, nz_sem)]
    for k in range(tiles):
        copies.append(pltpu.make_async_copy(amp_ref.at[:, k], source.at[k], sem.at[k]))
    for copy in copies:
        copy.start()

    n = pairs * GROUP
    row = lax.broadcasted_iota(jnp.int32, (n, n), 0)
    column = lax.broadcasted_iota(jnp.int32, (n, n), 1)
    turn = (row == column % GROUP * pairs + column // GROUP).astype(F32).astype(source.dtype)
    for copy in copies:
        copy.wait()

    def give(i, carry):
        for o in range(owners):
            j = o % GROUP
            rows = source[listed[start + i, o], :, o - j : o - j + GROUP].reshape(n, ct)
            block = jnp.dot(turn[j * pairs : (j + 1) * pairs], rows, preferred_element_type=F32)
            out_ref[o, i] = block.astype(out_ref.dtype)
        return carry

    lax.fori_loop(0, count, give, 0)


def pack(amplitudes, listed, first, count, by_task):
    pairs, tiles, owners, ct = amplitudes.shape
    anywhere = pl.BlockSpec(memory_space=pltpu.HBM)
    return pl.pallas_call(
        functools.partial(pack_kernel, by_task, first),
        in_specs=[anywhere, anywhere],
        out_specs=pl.BlockSpec(memory_space=pltpu.VMEM),
        out_shape=jax.ShapeDtypeStruct((owners, count, pairs, ct), amplitudes.dtype),
        scratch_shapes=[
            pltpu.SMEM(listed.shape, jnp.int32),
            pltpu.VMEM((tiles, pairs, owners, ct), amplitudes.dtype),
            pltpu.SemaphoreType.DMA,
            pltpu.SemaphoreType.DMA((tiles,)),
        ],
        compiler_params=pltpu.CompilerParams(vmem_limit_bytes=60 << 20),
        cost_estimate=pl.CostEstimate(
            flops=2 * count * owners * pairs * pairs * GROUP * ct * 8,
            bytes_accessed=2 * tiles * owners * pairs * ct,
            transcendentals=0,
        ),
        name="pack_shared" if by_task else "pack_direct",
    )(listed, amplitudes)


def product_kernel(counts, sides, on_top, inside, slots_ref, core_ref, places_ref, *refs):
    refs = list(refs)

    def take(n):
        taken = refs[:n]
        del refs[:n]
        return taken

    piece_refs, (int_ref,) = take(len(counts)), take(1)
    start_refs, out_refs = take(sides * on_top), take(sides)
    parts = out_refs if inside else take(sides)
    held, rhs, held_sem, rhs_sem, part_sem, out_sem = refs
    blocks, steps, pairs, tile = parts[0].shape
    where = [(piece, j) for piece, n in zip(piece_refs, counts, strict=True) for j in range(n)]
    slots = len(where)

    def columns(n):
        return pl.ds(n * tile if isinstance(n, int) else pl.multiple_of(n * tile, tile), tile)

    def fetch(n, l):
        return pltpu.make_async_copy(
            int_ref.at[slots_ref[l], 0, columns(n)], rhs.at[l, columns(n)], rhs_sem.at[n, l]
        )

    def fetch_rows(i, l):
        piece, j = where[l]
        return pltpu.make_async_copy(
            piece.at[:, core_ref[i], j], held.at[i, l], held_sem.at[i, l]
        )

    def fetch_start(n, i):
        return pltpu.make_async_copy(
            start_refs[i].at[:, n], parts[i].at[:, n], part_sem.at[n, i]
        )

    def put(n, i):
        return pltpu.make_async_copy(
            parts[i].at[:, n], out_refs[i].at[:, n], out_sem.at[n, i]
        )

    def bring(n, group):
        for l in group:
            fetch(n, l).start()
        if on_top and group[0] == 0:
            for i in range(sides):
                fetch_start(n, i).start()

    groups = [range(l, min(l + BUNDLE, slots)) for l in range(0, slots, BUNDLE)]

    def step(n, first):
        here = columns(n)
        total = [None] * sides
        for group in groups:
            for l in group:
                if first:
                    fetch_rows(0, l).wait()
                fetch(n, l).wait()

            @pl.when(n + 1 < steps)
            def _(group=group):
                bring(n + 1, group)

            for i in range(sides):
                for l in group:
                    if first and i > 0:
                        fetch_rows(i, l).wait()
                for l in group:
                    term = lax.dot_general(
                        held[i, l].reshape(blocks * pairs, -1),
                        rhs[l, here],
                        (((1,), (1,)), ((), ())),
                        preferred_element_type=F32,
                    )
                    total[i] = term if total[i] is None else total[i] + term
        for i in range(sides):
            sums = total[i].reshape(blocks, pairs, tile)
            if on_top:
                fetch_start(n, i).wait()
            for b in range(blocks):
                place = places_ref[i * blocks + b]
                parts[i][place, n] = sums[b] + parts[i][place, n] if on_top else sums[b]
            if not inside:
                put(n, i).start()

    for group in groups:
        for i in range(sides):
            for l in group:
                fetch_rows(i, l).start()
        bring(0, group)
    step(0, True)
    lax.fori_loop(1, steps, lambda n, carry: (step(n, False), carry)[1], 0)
    for n in range(0 if inside else steps):
        for i in range(sides):
            put(n, i).wait()


def product(pieces, integrals, slots, cores, places, start=(), spare=0, tile=512, name="product"):
    owners, _, pairs, ct = pieces[0].shape
    counts = [piece.shape[1] for piece in pieces]
    blocks, ab, sides, count = owners // 2, integrals.shape[2], cores.shape[0], sum(counts)
    pieces = [piece.reshape(blocks, 2, *piece.shape[1:]) for piece in pieces]
    small = pl.BlockSpec(memory_space=pltpu.SMEM)
    anywhere = pl.BlockSpec(memory_space=pl.ANY)
    whole = pl.BlockSpec(memory_space=pltpu.VMEM)
    steps, inside = ab // tile, spare > 0
    part = (blocks, steps, pairs, tile)
    return pl.pallas_call(
        functools.partial(product_kernel, counts, sides, len(start) > 0, inside),
        in_specs=[small] * 3 + [anywhere] * (len(pieces) + 1 + len(start)),
        out_specs=[whole if inside else anywhere] * sides,
        out_shape=[jax.ShapeDtypeStruct(part, F32)] * sides,
        scratch_shapes=[pltpu.VMEM(part, F32)] * (0 if inside else sides)
        + [
            pltpu.VMEM((sides, count, blocks, pairs, ct), pieces[0].dtype),
            pltpu.VMEM((count, ab, ct), integrals.dtype),
            pltpu.SemaphoreType.DMA((sides, count)),
            pltpu.SemaphoreType.DMA((steps, count)),
            pltpu.SemaphoreType.DMA((steps, sides)),
            pltpu.SemaphoreType.DMA((steps, sides)),
        ],
        compiler_params=pltpu.CompilerParams(vmem_limit_bytes=(60 << 20) - spare),
        cost_estimate=pl.CostEstimate(
            flops=2 * sides * blocks * pairs * ab * count * ct,
            bytes_accessed=ab * count * ct * 2 + sides * blocks * pairs * ab * 4,
            transcendentals=0,
        ),
        name=name,
    )(slots, cores, places, *pieces, integrals, *start)


def sum_to_first(part, swapped):
    def send(x, step):
        return lax.ppermute(x, "owner", along(step, swapped))

    return part[0] + send(part[1], 1) + send(part[3], 3) + send(part[2], 2)


def per_device(amplitudes, integrals, nonzero_tiles):
    owner = lax.axis_index("owner")
    task = lax.axis_index("task")
    y, z, c = owner // (2 * SIDE), owner // 2 % SIDE, owner % 2
    pairs = amplitudes.shape[0]
    ab = integrals.shape[2]
    mine = lax.dynamic_index_in_dim(nonzero_tiles, owner, 0, False)

    listed = nonzero_tiles.T
    live = listed.shape[0]
    shared = pack(amplitudes, listed, 0, QUARTER, True)
    quarter = lax.all_to_all(shared, "owner", 0, 0, tiled=True)
    direct = pack(amplitudes, listed, SHARED, live - SHARED, False)
    direct = lax.all_to_all(direct, "owner", 0, 0, tiled=True)
    before = lax.ppermute(quarter, "task", shift_task(1))
    after = lax.ppermute(quarter, "task", shift_task(-1))
    cut = QUARTER // 2
    across = [
        lax.ppermute(before[:, :cut], "task", shift_task(1)),
        lax.ppermute(after[:, cut:], "task", shift_task(-1)),
    ]

    def slots_of(t):
        return t % TASKS * QUARTER + jnp.arange(QUARTER)

    order = [slots_of(task), slots_of(task - 1), slots_of(task + 1), slots_of(task + 2)]
    slots = jnp.take(mine, jnp.concatenate([*order, jnp.arange(SHARED, live)]))
    near = 3 * QUARTER

    def places(core):
        dy = (jnp.repeat(jnp.arange(SIDE), SIDE) - y) % SIDE
        dz = (jnp.tile(jnp.arange(SIDE), SIDE) - z) % SIDE
        return jnp.where(core == 0, dz * SIDE + dy, dy * SIDE + dz)

    cores = jnp.stack([1 - c, c])
    where_to = jnp.concatenate([places(1 - c), places(c)])
    half = SIDE * SIDE
    both = product(
        [quarter, before, after], integrals, slots[:near], cores, where_to, name="product_near"
    )
    other, own = product(
        across, integrals, slots[near:SHARED], cores, where_to, both, name="product_across"
    )
    late = slots[SHARED:]
    (other,) = product(
        [direct], integrals, late, cores[:1], where_to[:half], [other], 6 << 20, name="product_other"
    )
    (own,) = product(
        [direct], integrals, late, cores[1:], where_to[half:], [own], 10 << 20, name="product_own"
    )
    swapped = lax.ppermute(other, "owner", owner_perm(lambda y, z, c: (y, z, 1 - c)))
    total = own + swapped
    total = sum_to_first(total.reshape(SIDE, SIDE, *total.shape[1:]), 0)
    total = sum_to_first(total, 1)
    return total.swapaxes(0, 1).reshape(pairs, ab)


def solution(mesh):
    placed = (P("owner", None, None, None), P(None, "owner", "task", None), P())
    return jax.shard_map(
        per_device, mesh=mesh, in_specs=placed, out_specs=P("owner", "task"), check_vma=False
    )
```

time: 275 us -> 138 us (0.50)
  waiting for transfers between devices: 190 us -> 43.3 us
  Pallas kernels: 0 us -> 56.4 us
  local copies, waits for them, and re-layouts: 41.6 us -> 4.29 us
  starting transfers between devices: 8.57 us -> 30.1 us
  matrix products: 21.4 us -> 0 us
  between operations: 13.4 us -> 0.34 us
    reduce_scatter x1 -> x0, waiting for transfers between devices: 98.5 us -> none  [per_device(): lax.psum_scatter(jnp.einsum('plx,lax->pa', received, int_live, preferred_...]
    all_to_all x1 -> x2, waiting for transfers between devices: 91 us -> 5.6 us  [the longest x1 3.85 us: per_device(): direct = lax.all_to_all(direct, 'owner', 0, 0, tiled=True)]
    pallas_call x0 -> x6, Pallas kernels: none -> 56.4 us  [the longest x4 38.7 us: product(): pl.pallas_call(functools.partial(product_kernel, counts, sides, len(start...]
    ppermute x0 -> x11, waiting for transfers between devices: none -> 37.7 us  [the longest x6 22.6 us: send(): return lax.ppermute(x, 'owner', along(step, swapped))]
    gather x2 -> x1, local copies, waits for them, and re-layouts: 23.4 us -> 0.7 us  [per_device(): slots = jnp.take(mine, jnp.concatenate([*order, jnp.arange(SHARED, live)]))]
    dot_general x1 -> x0, matrix products: 21.4 us -> none  [per_device(): jnp.einsum('plx,lax->pa', received, int_live, preferred_element_type=jnp....]
    ppermute x0 -> x11, starting transfers between devices: none -> 15.9 us  [the longest x6 8.97 us: send(): return lax.ppermute(x, 'owner', along(step, swapped))]
    unnamed x5 -> x18, local copies, waits for them, and re-layouts: 10.8 us -> 0.89 us
  transfers between devices with their start and end apart: 2 -> 13, of which waited for: 2 -> 8; matrix products, arithmetic and copies ran while one was open for 6% -> 3% of each run, Pallas kernels for 0% -> 29%
where the time goes in v1:
time: 138 us; the launch traced here: 137 us
  Pallas kernels  56.4 us (41%)
  waiting for transfers between devices  43.3 us (31%)
  starting transfers between devices  30.1 us (22%)
  local copies, waits for them, and re-layouts  4.29 us (3%)
  other arithmetic  2.54 us (2%)
    pallas_call x4, Pallas kernels, product(): pl.pallas_call(functools.partial(product_kernel, counts, sides, len(start...  38.7 us
    ppermute x6, waiting for transfers between devices, send(): return lax.ppermute(x, 'owner', along(step, swapped))  22.6 us
    pallas_call x2, Pallas kernels, pack(): pl.pallas_call(functools.partial(pack_kernel, by_task, first), in_specs=[...  17.8 us
    ppermute x1, waiting for transfers between devices, per_device(): before = lax.ppermute(quarter, 'task', shift_task(1))  15.1 us
    ppermute x6, starting transfers between devices, send(): return lax.ppermute(x, 'owner', along(step, swapped))  8.97 us
    all_to_all x1, starting transfers between devices, per_device(): quarter = lax.all_to_all(shared, 'owner', 0, 0, tiled=True)  8.43 us
    all_to_all x1, starting transfers between devices, per_device(): direct = lax.all_to_all(direct, 'owner', 0, 0, tiled=True)  5.78 us
    all_to_all x1, waiting for transfers between devices, per_device(): direct = lax.all_to_all(direct, 'owner', 0, 0, tiled=True)  3.85 us
  transfers between devices with their start and end apart: 13, of which 8 were waited for; matrix products, arithmetic and copies ran while one was open for 3% of the time, Pallas kernels for 29%

profile of v1, /device:TPU:0, one launch (start us, length us, event | category | flops | bytes accessed | tf_op | source)
XLA Modules:
  0.0 137.1 jit_solution(1467542248577554140)
XLA Ops:
  0.0 5.7 %pack_shared.1 = bf16[32,2,24,256]{3,2,1,0:T(8,128)(2,1)} custom-call(s32[18,32]{1,0:T(8,128)} %bitcast.47, bf16[24,20,32,256]{3,2,1,0:T(8,128)(2,1)} %amp_ref.3), custom_call_target="tpu_custom_call" | custom-call | flops 1207959552 | bytes 7864320 | tf_op jit(solution)/shard_map/pack_shared/pallas_call | solution.py:72
  5.7 8.4 %all-to-all-start.1 = ((bf16[32,2,24,256]{3,2,1,0:T(8,128)(2,1)}), bf16[32,2,24,256]{3,2,1,0:T(8,128)(2,1)S(1)}, u32[]{:S(2)}, u32[]{:S(2)}) async-start(bf16[32,2,24,256]{3,2,1,0:T(8,128)(2,1)} %pack_shared.1), calls=%async_computation.1 | async-start | bytes 1572864 | tf_op jit(solution)/shard_map/all_to_all | solution.py:241
  14.1 12.1 %pack_direct.1 = bf16[32,10,24,256]{3,2,1,0:T(8,128)(2,1)} custom-call(s32[18,32]{1,0:T(8,128)} %bitcast.48, bf16[24,20,32,256]{3,2,1,0:T(8,128)(2,1)} %amp_ref.3), custom_call_target="tpu_custom_call" | custom-call | flops 6039797760 | bytes 7864320 | tf_op jit(solution)/shard_map/pack_direct/pallas_call | solution.py:72
  26.2 0.0 copy-start.6
  26.2 1.7 %all-to-all-done.1 = bf16[32,2,24,256]{3,2,1,0:T(8,128)(2,1)S(1)} async-done(((bf16[32,2,24,256]{3,2,1,0:T(8,128)(2,1)}), bf16[32,2,24,256]{3,2,1,0:T(8,128)(2,1)S(1)}, u32[]{:S(2)}, u32[]{:S(2)}) %all-to-all-start.1) | async-done | bytes 786464 | tf_op jit(solution)/shard_map/all_to_all | solution.py:241
  28.0 5.8 %all-to-all-start = ((bf16[32,10,24,256]{3,2,1,0:T(8,128)(2,1)}), bf16[32,10,24,256]{3,2,1,0:T(8,128)(2,1)}, u32[]{:S(2)}, u32[]{:S(2)}) async-start(bf16[32,10,24,256]{3,2,1,0:T(8,128)(2,1)} %pack_direct.1), calls=%async_computation | async-start | bytes 7864320 | tf_op jit(solution)/shard_map/all_to_all | solution.py:243
  33.9 0.1 concatenate.45
  34.0 0.2 dynamic-slice_reduce_fusion
  34.2 0.7 gather_fusion
  34.9 0.1 concatenate.39
  35.0 1.6 %collective-permute-start = (bf16[32,2,24,256]{3,2,1,0:T(8,128)(2,1)S(1)}, bf16[32,2,24,256]{3,2,1,0:T(8,128)(2,1)S(1)}, u32[]{:S(2)}, u32[]{:S(2)}) collective-permute-start(bf16[32,2,24,256]{3,2,1,0:T(8,128)(2,1)S(1)} %all-to-all-done.1), channel_id=1, source_target_pairs={{0,1},{1,2},{2,3},{3,0},{4,5},{5,6},{6,7},{7,4},{8,9},{9,10},{10,1... | collective-permute-start | bytes 2359304 | tf_op jit(solution)/shard_map/ppermute | solution.py:244
  36.6 1.7 %collective-permute-start.2 = (bf16[32,2,24,256]{3,2,1,0:T(8,128)(2,1)S(1)}, bf16[32,2,24,256]{3,2,1,0:T(8,128)(2,1)S(1)}, u32[]{:S(2)}, u32[]{:S(2)}) collective-permute-start(bf16[32,2,24,256]{3,2,1,0:T(8,128)(2,1)S(1)} %all-to-all-done.1), channel_id=1, source_target_pairs={{0,3},{1,0},{2,1},{3,2},{4,7},{5,4},{6,5},{7,6},{8,11},{9,8},{10,9... | collective-permute-start | bytes 2359304 | tf_op jit(solution)/shard_map/ppermute | solution.py:245
  38.3 0.6 slice.44.slots_ref
  38.9 0.6 slice.43.slots_ref
  39.5 0.1 sub.40
  39.6 0.1 sub.44
  39.7 0.6 pad_add_fusion.1.places_ref
  40.2 0.6 pad_add_fusion.core_ref
  40.8 15.1 %collective-permute-done = bf16[32,2,24,256]{3,2,1,0:T(8,128)(2,1)S(1)} collective-permute-done((bf16[32,2,24,256]{3,2,1,0:T(8,128)(2,1)S(1)}, bf16[32,2,24,256]{3,2,1,0:T(8,128)(2,1)S(1)}, u32[]{:S(2)}, u32[]{:S(2)}) %collective-permute-start) | collective-permute-done | bytes 786464 | tf_op jit(solution)/shard_map/ppermute | solution.py:244
  56.0 0.3 collective-permute-start.1
  56.3 0.0 collective-permute-done.2
  56.4 3.0 %collective-permute-start.3 = (bf16[32,1,24,256]{3,2,1,0:T(8,128)(2,1)S(1)}, bf16[32,1,24,256]{3,2,1,0:T(8,128)(2,1)S(1)}, u32[]{:S(2)}, u32[]{:S(2)}) collective-permute-start(bf16[32,1,24,256]{3,2,1,0:T(8,128)(2,1)S(1)} %slice.59), channel_id=1, source_target_pairs={{0,3},{1,0},{2,1},{3,2},{4,7},{5,4},{6,5},{7,6},{8,11},{9,8},{10,9... | collective-permute-start | bytes 1179656 | tf_op jit(solution)/shard_map/ppermute | solution.py:249
  59.4 10.9 %product_near.1 = (f32[16,4,24,512]{3,2,1,0:T(8,128)}, f32[16,4,24,512]{3,2,1,0:T(8,128)}) custom-call(s32[6]{0:T(128)} %bitcast.49, s32[2]{0:T(128)} %pad_add_fusion.core_ref, s32[32]{0:T(128)} %pad_add_fusion.1.places_ref, bf16[16,2,2,24,256]{4,3,2,1,0:T(8,128)(2,1)} %bitcast.42, bf16[16,2,2,24,256]{4,3,2,1,0:T(8,128)(2,1)} %bitcast.43, ...), custom_call_target="tpu_custom_call" | custom-call | flops 4831838208 | bytes 12582912 | tf_op jit(solution)/shard_map/product_near/pallas_call | solution.py:199
  70.3 0.0 collective-permute-done.1
  70.3 0.0 collective-permute-done.3
  70.3 0.7 copy-done.4
  71.0 0.1 copy-done.5
  71.2 8.4 %product_across.1 = (f32[16,4,24,512]{3,2,1,0:T(8,128)}, f32[16,4,24,512]{3,2,1,0:T(8,128)}) custom-call(s32[2]{0:T(128)} %slice.44.slots_ref, s32[2]{0:T(128)} %pad_add_fusion.core_ref, s32[32]{0:T(128)} %pad_add_fusion.1.places_ref, bf16[16,2,1,24,256]{4,3,2,1,0:T(8,128)(2,1)} %bitcast.45, bf16[16,2,1,24,256]{4,3,2,1,0:T(8,128)(2,1)} %bitcast.46, ...), custom_call_target="tpu_custom_call" | custom-call | flops 1610612736 | bytes 8388608 | tf_op jit(solution)/shard_map/product_across/pallas_call | solution.py:199
  79.6 3.9 %all-to-all-done = bf16[32,10,24,256]{3,2,1,0:T(8,128)(2,1)} async-done(((bf16[32,10,24,256]{3,2,1,0:T(8,128)(2,1)}), bf16[32,10,24,256]{3,2,1,0:T(8,128)(2,1)}, u32[]{:S(2)}, u32[]{:S(2)}) %all-to-all-start) | async-done | bytes 3932192 | tf_op jit(solution)/shard_map/all_to_all | solution.py:243
  83.4 10.7 %product_other.1 = f32[16,4,24,512]{3,2,1,0:T(8,128)} custom-call(s32[10]{0:T(128)} %slice.43.slots_ref, s32[1]{0:T(128)} %bitcast.9.core_ref, s32[16]{0:T(128)} %copy-done.7, bf16[16,2,10,24,256]{4,3,2,1,0:T(8,128)(2,1)} %bitcast.8.refs_0_, bf16[20,1,2048,256]{3,2,1,0:T(8,128)(2,1)} %refs_1_.3, f32[16,4,24,512]{3,2,1,0:T(8,128)} %get-tuple-element.12.refs_2_), custom_call_target="tpu_custom_call" | custom-call | flops 4026531840 | bytes 13631488 | tf_op jit(solution)/shard_map/product_other/pallas_call | solution.py:199
  94.1 0.3 collective-permute-start.4
  94.4 8.7 %product_own.1 = f32[16,4,24,512]{3,2,1,0:T(8,128)S(1)} custom-call(s32[10]{0:T(128)S(1)} %copy-done, s32[1]{0:T(128)} %bitcast.6.core_ref, s32[16]{0:T(128)S(1)} %broadcast_select_fusion.1.places_ref, bf16[16,2,10,24,256]{4,3,2,1,0:T(8,128)(2,1)} %bitcast.8.refs_0_, bf16[20,1,2048,256]{3,2,1,0:T(8,128)(2,1)} %refs_1_.3, ...), custom_call_target="tpu_custom_call" | custom-call | flops 4026531840 | bytes 13631488 | tf_op jit(solution)/shard_map/product_own/pallas_call | solution.py:199
  103.1 0.9 add.203
  104.0 0.2 fusion.14
  104.3 2.6 %collective-permute-start.5 = (f32[4,4,24,512]{3,2,1,0:T(8,128)S(1)}, f32[4,4,24,512]{3,2,1,0:T(8,128)S(1)}, u32[]{:S(2)}, u32[]{:S(2)}) collective-permute-start(f32[4,4,24,512]{3,2,1,0:T(8,128)S(1)} %get-tuple-element.16), channel_id=1, source_target_pairs={{0,8},{4,36},{8,16},{12,44},{16,24},{20,52},{24,0},{28,60},{32,40}... | collective-permute-start | bytes 2359304 | tf_op jit(solution)/shard_map/ppermute | solution.py:225
  106.9 0.7 collective-permute-start.6
  107.6 1.5 %collective-permute-start.7 = (f32[4,4,24,512]{3,2,1,0:T(8,128)S(1)}, f32[4,4,24,512]{3,2,1,0:T(8,128)S(1)}, u32[]{:S(2)}, u32[]{:S(2)}) collective-permute-start(f32[4,4,24,512]{3,2,1,0:T(8,128)S(1)} %get-tuple-element.17), channel_id=1, source_target_pairs={{0,16},{4,68},{8,24},{12,76},{16,0},{20,84},{24,8},{28,92},{32,48}... | collective-permute-start | bytes 2359304 | tf_op jit(solution)/shard_map/ppermute | solution.py:225
  109.1 8.5 %collective-permute-done.5 = f32[4,4,24,512]{3,2,1,0:T(8,128)S(1)} collective-permute-done((f32[4,4,24,512]{3,2,1,0:T(8,128)S(1)}, f32[4,4,24,512]{3,2,1,0:T(8,128)S(1)}, u32[]{:S(2)}, u32[]{:S(2)}) %collective-permute-start.5) | collective-permute-done | bytes 786464 | tf_op jit(solution)/shard_map/ppermute | solution.py:225
  117.6 1.3 collective-permute-done.6
  118.9 7.6 %collective-permute-done.7 = f32[4,4,24,512]{3,2,1,0:T(8,128)S(1)} collective-permute-done((f32[4,4,24,512]{3,2,1,0:T(8,128)S(1)}, f32[4,4,24,512]{3,2,1,0:T(8,128)S(1)}, u32[]{:S(2)}, u32[]{:S(2)}) %collective-permute-start.7) | collective-permute-done | bytes 786464 | tf_op jit(solution)/shard_map/ppermute | solution.py:225
  126.5 0.4 fusion.1
  126.9 1.0 collective-permute-start.10
  127.9 1.5 %collective-permute-start.8 = (f32[4,24,512]{2,1,0:T(8,128)S(1)}, f32[4,24,512]{2,1,0:T(8,128)S(1)}, u32[]{:S(2)}, u32[]{:S(2)}) collective-permute-start(f32[4,24,512]{2,1,0:T(8,128)S(1)} %get-tuple-element.19), channel_id=1, source_target_pairs={{0,32},{4,12},{8,40},{12,20},{16,48},{20,28},{24,56},{28,4},{32,64... | collective-permute-start | bytes 589832 | tf_op jit(solution)/shard_map/ppermute | solution.py:225
  129.4 1.8 %collective-permute-start.9 = (f32[4,24,512]{2,1,0:T(8,128)S(1)}, f32[4,24,512]{2,1,0:T(8,128)S(1)}, u32[]{:S(2)}, u32[]{:S(2)}) collective-permute-start(f32[4,24,512]{2,1,0:T(8,128)S(1)} %get-tuple-element.21), channel_id=1, source_target_pairs={{0,96},{4,28},{8,104},{12,4},{16,112},{20,12},{24,120},{28,20},{32... | collective-permute-start | bytes 589832 | tf_op jit(solution)/shard_map/ppermute | solution.py:225
  131.1 3.2 %collective-permute-done.10 = f32[4,24,512]{2,1,0:T(8,128)S(1)} collective-permute-done((f32[4,24,512]{2,1,0:T(8,128)S(1)}, f32[4,24,512]{2,1,0:T(8,128)S(1)}, u32[]{:S(2)}, u32[]{:S(2)}) %collective-permute-start.10) | collective-permute-done | bytes 196640 | tf_op jit(solution)/shard_map/ppermute | solution.py:225
  134.3 2.0 %collective-permute-done.8 = f32[4,24,512]{2,1,0:T(8,128)S(1)} collective-permute-done((f32[4,24,512]{2,1,0:T(8,128)S(1)}, f32[4,24,512]{2,1,0:T(8,128)S(1)}, u32[]{:S(2)}, u32[]{:S(2)}) %collective-permute-start.8) | collective-permute-done | bytes 196640 | tf_op jit(solution)/shard_map/ppermute | solution.py:225
  136.3 0.1 fusion.5
  136.4 0.7 copy.5
  (33 shorter events, 0.2 us)
Async XLA Ops:
  5.7 22.3 %all-to-all-start.1 = ((bf16[32,2,24,256]{3,2,1,0:T(8,128)(2,1)}), bf16[32,2,24,256]{3,2,1,0:T(8,128)(2,1)S(1)}, u32[]{:S(2)}, u32[]{:S(2)}) async-start(bf16[32,2,24,256]{3,2,1,0:T(8,128)(2,1)} %pack_shared.1), calls=%async_computation.1 | async-start | bytes 1572864 | tf_op jit(solution)/shard_map/all_to_all | solution.py:241
  26.2 7.8 %copy-start.6 = (s32[32,18]{0,1:T(8,128)S(1)}, s32[32,18]{0,1:T(8,128)}, u32[]{:S(2)}) copy-start(s32[32,18]{0,1:T(8,128)} %param.5) | copy-start | bytes 6916
  28.0 8.6 %copy-start.1 = (bf16[32,2,24,256]{3,2,1,0:T(8,128)(2,1)}, bf16[32,2,24,256]{3,2,1,0:T(8,128)(2,1)S(1)}, u32[]{:S(2)}) copy-start(bf16[32,2,24,256]{3,2,1,0:T(8,128)(2,1)S(1)} %all-to-all-done.1) | copy-start | bytes 2359300
  28.0 55.5 %all-to-all-start = ((bf16[32,10,24,256]{3,2,1,0:T(8,128)(2,1)}), bf16[32,10,24,256]{3,2,1,0:T(8,128)(2,1)}, u32[]{:S(2)}, u32[]{:S(2)}) async-start(bf16[32,10,24,256]{3,2,1,0:T(8,128)(2,1)} %pack_direct.1), calls=%async_computation | async-start | bytes 7864320 | tf_op jit(solution)/shard_map/all_to_all | solution.py:243
  35.0 24.4 %copy-start.8 = (s32[18]{0:T(128)}, s32[18]{0:T(128)S(1)}, u32[]{:S(2)}) copy-start(s32[18]{0:T(128)S(1)} %and_select_fusion.2) | copy-start | bytes 220
  35.0 20.9 %collective-permute-start = (bf16[32,2,24,256]{3,2,1,0:T(8,128)(2,1)S(1)}, bf16[32,2,24,256]{3,2,1,0:T(8,128)(2,1)S(1)}, u32[]{:S(2)}, u32[]{:S(2)}) collective-permute-start(bf16[32,2,24,256]{3,2,1,0:T(8,128)(2,1)S(1)} %all-to-all-done.1), channel_id=1, source_target_pairs={{0,1},{1,2},{2,3},{3,0},{4,5},{5,6},{6,7},{7,4},{8,9},{9,10},{10,1... | collective-permute-start | bytes 2359304 | tf_op jit(solution)/shard_map/ppermute | solution.py:244
  36.6 19.8 %collective-permute-start.2 = (bf16[32,2,24,256]{3,2,1,0:T(8,128)(2,1)S(1)}, bf16[32,2,24,256]{3,2,1,0:T(8,128)(2,1)S(1)}, u32[]{:S(2)}, u32[]{:S(2)}) collective-permute-start(bf16[32,2,24,256]{3,2,1,0:T(8,128)(2,1)S(1)} %all-to-all-done.1), channel_id=1, source_target_pairs={{0,3},{1,0},{2,1},{3,2},{4,7},{5,4},{6,5},{7,6},{8,11},{9,8},{10,9... | collective-permute-start | bytes 2359304 | tf_op jit(solution)/shard_map/ppermute | solution.py:245
  39.7 30.6 %copy-start.7 = (s32[16]{0:T(128)}, s32[16]{0:T(128)S(1)}, u32[]{:S(2)}) copy-start(s32[16]{0:T(128)S(1)} %get-tuple-element.13.places_ref) | copy-start | bytes 196
  55.9 3.4 %copy-start.2 = (bf16[32,2,24,256]{3,2,1,0:T(8,128)(2,1)}, bf16[32,2,24,256]{3,2,1,0:T(8,128)(2,1)S(1)}, u32[]{:S(2)}) copy-start(bf16[32,2,24,256]{3,2,1,0:T(8,128)(2,1)S(1)} %collective-permute-done) | copy-start | bytes 2359300
  56.0 14.3 %collective-permute-start.1 = (bf16[32,1,24,256]{3,2,1,0:T(8,128)(2,1)S(1)}, bf16[32,1,24,256]{3,2,1,0:T(8,128)(2,1)S(1)}, u32[]{:S(2)}, u32[]{:S(2)}) collective-permute-start(bf16[32,1,24,256]{3,2,1,0:T(8,128)(2,1)S(1)} %slice.58), channel_id=1, source_target_pairs={{0,1},{1,2},{2,3},{3,0},{4,5},{5,6},{6,7},{7,4},{8,9},{9,10},{10,1... | collective-permute-start | bytes 1179656 | tf_op jit(solution)/shard_map/ppermute | solution.py:248
  56.3 3.1 %copy-start.3 = (bf16[32,2,24,256]{3,2,1,0:T(8,128)(2,1)}, bf16[32,2,24,256]{3,2,1,0:T(8,128)(2,1)S(1)}, u32[]{:S(2)}) copy-start(bf16[32,2,24,256]{3,2,1,0:T(8,128)(2,1)S(1)} %collective-permute-done.2) | copy-start | bytes 2359300
  56.4 13.9 %collective-permute-start.3 = (bf16[32,1,24,256]{3,2,1,0:T(8,128)(2,1)S(1)}, bf16[32,1,24,256]{3,2,1,0:T(8,128)(2,1)S(1)}, u32[]{:S(2)}, u32[]{:S(2)}) collective-permute-start(bf16[32,1,24,256]{3,2,1,0:T(8,128)(2,1)S(1)} %slice.59), channel_id=1, source_target_pairs={{0,3},{1,0},{2,1},{3,2},{4,7},{5,4},{6,5},{7,6},{8,11},{9,8},{10,9... | collective-permute-start | bytes 1179656 | tf_op jit(solution)/shard_map/ppermute | solution.py:249
  70.3 0.8 copy-start.4
  70.3 0.9 copy-start.5
  83.4 11.0 %copy-start = (s32[10]{0:T(128)S(1)}, s32[10]{0:T(128)}, u32[]{:S(2)}) copy-start(s32[10]{0:T(128)} %slice.43.slots_ref) | copy-start | bytes 124
  94.1 9.0 %collective-permute-start.4 = (f32[16,4,24,512]{3,2,1,0:T(8,128)}, f32[16,4,24,512]{3,2,1,0:T(8,128)S(1)}, u32[]{:S(2)}, u32[]{:S(2)}) collective-permute-start(f32[16,4,24,512]{3,2,1,0:T(8,128)} %product_other.1), channel_id=1, source_target_pairs={{0,4},{4,0},{8,12},{12,8},{16,20},{20,16},{24,28},{28,24},{32,36},... | collective-permute-start | bytes 9437192 | tf_op jit(solution)/shard_map/ppermute | solution.py:280
  104.3 13.3 %collective-permute-start.5 = (f32[4,4,24,512]{3,2,1,0:T(8,128)S(1)}, f32[4,4,24,512]{3,2,1,0:T(8,128)S(1)}, u32[]{:S(2)}, u32[]{:S(2)}) collective-permute-start(f32[4,4,24,512]{3,2,1,0:T(8,128)S(1)} %get-tuple-element.16), channel_id=1, source_target_pairs={{0,8},{4,36},{8,16},{12,44},{16,24},{20,52},{24,0},{28,60},{32,40}... | collective-permute-start | bytes 2359304 | tf_op jit(solution)/shard_map/ppermute | solution.py:225
  106.9 12.0 %collective-permute-start.6 = (f32[4,4,24,512]{3,2,1,0:T(8,128)S(1)}, f32[4,4,24,512]{3,2,1,0:T(8,128)S(1)}, u32[]{:S(2)}, u32[]{:S(2)}) collective-permute-start(f32[4,4,24,512]{3,2,1,0:T(8,128)S(1)} %get-tuple-element.18), channel_id=1, source_target_pairs={{0,24},{4,100},{8,0},{12,108},{16,8},{20,116},{24,16},{28,124},{32... | collective-permute-start | bytes 2359304 | tf_op jit(solution)/shard_map/ppermute | solution.py:225
  107.6 18.9 %collective-permute-start.7 = (f32[4,4,24,512]{3,2,1,0:T(8,128)S(1)}, f32[4,4,24,512]{3,2,1,0:T(8,128)S(1)}, u32[]{:S(2)}, u32[]{:S(2)}) collective-permute-start(f32[4,4,24,512]{3,2,1,0:T(8,128)S(1)} %get-tuple-element.17), channel_id=1, source_target_pairs={{0,16},{4,68},{8,24},{12,76},{16,0},{20,84},{24,8},{28,92},{32,48}... | collective-permute-start | bytes 2359304 | tf_op jit(solution)/shard_map/ppermute | solution.py:225
  126.9 7.4 %collective-permute-start.10 = (f32[4,24,512]{2,1,0:T(8,128)S(1)}, f32[4,24,512]{2,1,0:T(8,128)S(1)}, u32[]{:S(2)}, u32[]{:S(2)}) collective-permute-start(f32[4,24,512]{2,1,0:T(8,128)S(1)} %get-tuple-element.20), channel_id=1, source_target_pairs={{0,64},{4,20},{8,72},{12,28},{16,80},{20,4},{24,88},{28,12},{32,96... | collective-permute-start | bytes 589832 | tf_op jit(solution)/shard_map/ppermute | solution.py:225
  127.9 8.4 %collective-permute-start.8 = (f32[4,24,512]{2,1,0:T(8,128)S(1)}, f32[4,24,512]{2,1,0:T(8,128)S(1)}, u32[]{:S(2)}, u32[]{:S(2)}) collective-permute-start(f32[4,24,512]{2,1,0:T(8,128)S(1)} %get-tuple-element.19), channel_id=1, source_target_pairs={{0,32},{4,12},{8,40},{12,20},{16,48},{20,28},{24,56},{28,4},{32,64... | collective-permute-start | bytes 589832 | tf_op jit(solution)/shard_map/ppermute | solution.py:225
  129.4 6.9 %collective-permute-start.9 = (f32[4,24,512]{2,1,0:T(8,128)S(1)}, f32[4,24,512]{2,1,0:T(8,128)S(1)}, u32[]{:S(2)}, u32[]{:S(2)}) collective-permute-start(f32[4,24,512]{2,1,0:T(8,128)S(1)} %get-tuple-element.21), channel_id=1, source_target_pairs={{0,96},{4,28},{8,104},{12,4},{16,112},{20,12},{24,120},{28,20},{32... | collective-permute-start | bytes 589832 | tf_op jit(solution)/shard_map/ppermute | solution.py:225

commit v2 on v1

v2 whole, which is shorter than its diff:
```python
import functools

import jax
import jax.numpy as jnp
from jax import lax
from jax.experimental import pallas as pl
from jax.experimental.pallas import tpu as pltpu
from jax.sharding import PartitionSpec as P

OWNERS, TASKS, SIDE = 32, 4, 4
WHOLE, HALVES, LANES = 2, 2, 128
UNITS = WHOLE * HALVES + 1
SHARED = UNITS * TASKS // HALVES
BUNDLE = 5
GROUP = 8
F32 = jnp.float32


def owner_at(y, z, c):
    return ((y % SIDE) * SIDE + z % SIDE) * 2 + c


def owner_perm(move):
    return [
        (owner_at(y, z, c), owner_at(*move(y, z, c)))
        for y in range(SIDE)
        for z in range(SIDE)
        for c in range(2)
    ]


def along(step, cores_swapped):
    return owner_perm(
        lambda y, z, c: (y, z + step, c) if c == cores_swapped else (y + step, z, c)
    )


def shift_task(step):
    return [(t, (t + step) % TASKS) for t in range(TASKS)]


def pack_kernel(by_task, nz_ref, amp_ref, out_ref, listed, source, nz_sem, sem):
    owners, count, pairs, _ = out_ref.shape
    tiles, _, _, ct = source.shape
    task = lax.axis_index("task")
    copies = [pltpu.make_async_copy(nz_ref, listed, nz_sem)]
    for k in range(tiles):
        copies.append(pltpu.make_async_copy(amp_ref.at[:, k], source.at[k], sem.at[k]))
    for copy in copies:
        copy.start()

    n = pairs * GROUP
    row = lax.broadcasted_iota(jnp.int32, (n, n), 0)
    column = lax.broadcasted_iota(jnp.int32, (n, n), 1)
    turn = (row == column % GROUP * pairs + column // GROUP).astype(F32).astype(source.dtype)
    for copy in copies:
        copy.wait()

    def block(o, slot):
        j = o % GROUP
        rows = source[listed[slot, o], :, o - j : o - j + GROUP].reshape(n, ct)
        product = jnp.dot(turn[j * pairs : (j + 1) * pairs], rows, preferred_element_type=F32)
        return product.astype(out_ref.dtype)

    def give(i, carry):
        for o in range(owners):
            out_ref[o, i] = block(o, SHARED + i)
        return carry

    def give_units(i, carry):
        for o in range(owners):
            both = block(o, task * WHOLE + i)
            for h in range(HALVES):
                out_ref[o, HALVES * i + h] = both[:, h * LANES : (h + 1) * LANES]
        return carry

    if not by_task:
        lax.fori_loop(0, count, give, 0)
        return
    lax.fori_loop(0, WHOLE, give_units, 0)
    for o in range(owners):
        both = block(o, TASKS * WHOLE + task // HALVES)
        halves = [both[:, h * LANES : (h + 1) * LANES] for h in range(HALVES)]
        out_ref[o, UNITS - 1] = jnp.where(task % HALVES == 0, *halves)


def pack(amplitudes, listed, by_task):
    pairs, tiles, owners, ct = amplitudes.shape
    count, width = (UNITS, LANES) if by_task else (listed.shape[0] - SHARED, ct)
    anywhere = pl.BlockSpec(memory_space=pltpu.HBM)
    return pl.pallas_call(
        functools.partial(pack_kernel, by_task),
        in_specs=[anywhere, anywhere],
        out_specs=pl.BlockSpec(memory_space=pltpu.VMEM),
        out_shape=jax.ShapeDtypeStruct((owners, count, pairs, width), amplitudes.dtype),
        scratch_shapes=[
            pltpu.SMEM(listed.shape, jnp.int32),
            pltpu.VMEM((tiles, pairs, owners, ct), amplitudes.dtype),
            pltpu.SemaphoreType.DMA,
            pltpu.SemaphoreType.DMA((tiles,)),
        ],
        compiler_params=pltpu.CompilerParams(vmem_limit_bytes=60 << 20),
        cost_estimate=pl.CostEstimate(
            flops=2 * count * owners * pairs * pairs * GROUP * ct * 8,
            bytes_accessed=2 * tiles * owners * pairs * ct,
            transcendentals=0,
        ),
        name="pack_shared" if by_task else "pack_direct",
    )(listed, amplitudes)


def product_kernel(pieces, plan, sides, on_top, cuts, slots_ref, half_ref, core_ref, places_ref, *refs):
    refs = list(refs)

    def take(n):
        taken = refs[:n]
        del refs[:n]
        return taken

    piece_refs, (int_ref,) = take(pieces), take(1)
    start_refs, out_refs, parts = take(sides * on_top), take(sides * len(cuts)), take(sides)
    held, rhs, held_sem, rhs_sem, part_sem, out_sem = refs
    blocks, pairs, ab = parts[0].shape
    steps = rhs_sem.shape[0]
    tile = ab // steps
    slots = len(plan)

    def columns(n):
        return pl.ds(n * tile if isinstance(n, int) else pl.multiple_of(n * tile, tile), tile)

    def fetches(n, l):
        if l < slots - 1:
            yield pltpu.make_async_copy(
                int_ref.at[slots_ref[l], 0, columns(n)], rhs.at[l, columns(n)], rhs_sem.at[n, l]
            )
            return
        for h in range(HALVES):
            lanes = pl.ds(pl.multiple_of(half_ref[h] * LANES, LANES), LANES)
            yield pltpu.make_async_copy(
                int_ref.at[slots_ref[l + h], 0, columns(n), lanes],
                rhs.at[l, columns(n), h * LANES : (h + 1) * LANES],
                rhs_sem.at[n, l + h],
            )

    def rows(i, l):
        for m, (p, j, part, parts_in_all, h) in enumerate(plan[l]):
            share = blocks // parts_in_all
            to = held.at[l, pl.ds(i * blocks + part * share, share)]
            if h is not None:
                to = to.at[:, :, h * LANES : (h + 1) * LANES]
            yield pltpu.make_async_copy(piece_refs[p].at[:, core_ref[i], j], to, held_sem.at[i, l, m])

    def fetch_start(n, i):
        return pltpu.make_async_copy(
            start_refs[i].at[:, :, columns(n)], parts[i].at[:, :, columns(n)], part_sem.at[n, i]
        )

    def puts(n, i):
        first = 0
        for k, size in enumerate(cuts):
            yield pltpu.make_async_copy(
                parts[i].at[first : first + size, :, columns(n)],
                out_refs[i * len(cuts) + k].at[:, :, columns(n)],
                out_sem.at[n, i, k],
            )
            first += size

    def bring(n, group):
        for l in group:
            for copy in fetches(n, l):
                copy.start()
        if on_top and group[0] == 0:
            for i in range(sides):
                fetch_start(n, i).start()

    groups = [range(l, min(l + BUNDLE, slots)) for l in range(0, slots, BUNDLE)]

    def step(n, first):
        here = columns(n)
        total = None
        for group in groups:
            for l in group:
                if first:
                    for i in range(sides):
                        for copy in rows(i, l):
                            copy.wait()
                for copy in fetches(n, l):
                    copy.wait()

            @pl.when(n + 1 < steps)
            def _(group=group):
                bring(n + 1, group)

            for l in group:
                term = lax.dot_general(
                    held[l].reshape(sides * blocks * pairs, -1),
                    rhs[l, here],
                    (((1,), (1,)), ((), ())),
                    preferred_element_type=F32,
                )
                total = term if total is None else total + term
        total = total.reshape(sides, blocks, pairs, tile)
        for i in range(sides):
            sums = total[i]
            if on_top:
                fetch_start(n, i).wait()
            for b in range(blocks):
                place = places_ref[i * blocks + b]
                before = parts[i][place, :, here] if on_top else 0
                parts[i][place, :, here] = sums[b] + before
            for copy in puts(n, i):
                copy.start()

    for group in groups:
        for i in range(sides):
            for l in group:
                for copy in rows(i, l):
                    copy.start()
        bring(0, group)
    step(0, True)
    lax.fori_loop(1, steps, lambda n, carry: (step(n, False), carry)[1], 0)
    for n in range(steps):
        for i in range(sides):
            for copy in puts(n, i):
                copy.wait()


def product(pieces, plan, integrals, slots, half, cores, places, start=(), cuts=None, spare=0, tile=512, name="product"):
    ab, ct = integrals.shape[2:]
    blocks, pairs, sides, count = OWNERS // 2, pieces[0].shape[2], cores.shape[0], len(plan)
    pieces = [piece.reshape(piece.shape[0] // 2, 2, *piece.shape[1:]) for piece in pieces]
    small = pl.BlockSpec(memory_space=pltpu.SMEM)
    anywhere = pl.BlockSpec(memory_space=pl.ANY)
    steps, cuts = ab // tile, cuts or (blocks,)
    part = (blocks, pairs, ab)
    return pl.pallas_call(
        functools.partial(product_kernel, len(pieces), plan, sides, len(start) > 0, cuts),
        in_specs=[small] * 4 + [anywhere] * (len(pieces) + 1 + len(start)),
        out_specs=[anywhere] * (sides * len(cuts)),
        out_shape=[jax.ShapeDtypeStruct((size, *part[1:]), F32) for size in cuts] * sides,
        scratch_shapes=[pltpu.VMEM(part, F32)] * sides
        + [
            pltpu.VMEM((count, sides * blocks, pairs, ct), integrals.dtype),
            pltpu.VMEM((count, ab, ct), integrals.dtype),
            pltpu.SemaphoreType.DMA((sides, count, max(map(len, plan)))),
            pltpu.SemaphoreType.DMA((steps, count + 1)),
            pltpu.SemaphoreType.DMA((steps, sides)),
            pltpu.SemaphoreType.DMA((steps, sides, len(cuts))),
        ],
        compiler_params=pltpu.CompilerParams(vmem_limit_bytes=(60 - spare) << 20),
        cost_estimate=pl.CostEstimate(
            flops=2 * sides * blocks * pairs * ab * count * ct,
            bytes_accessed=ab * count * ct * 2 + sides * blocks * pairs * ab * 4,
            transcendentals=0,
        ),
        name=name,
    )(slots, half, cores, places, *pieces, integrals, *start)


def send(x, step, swapped=0):
    return lax.ppermute(x, "owner", along(step, swapped))


def trade(x):
    return lax.ppermute(x, "owner", owner_perm(lambda y, z, c: (y, z, 1 - c)))


def per_device(amplitudes, integrals, nonzero_tiles):
    owner = lax.axis_index("owner")
    task = lax.axis_index("task")
    y, z, c = owner // (2 * SIDE), owner // 2 % SIDE, owner % 2
    pairs = amplitudes.shape[0]
    ab = integrals.shape[2]
    mine = lax.dynamic_index_in_dim(nonzero_tiles, owner, 0, False)

    listed = nonzero_tiles.T
    live = listed.shape[0]
    shared = pack(amplitudes, listed, True)
    quarter = lax.all_to_all(shared, "owner", 0, 0, tiled=True)
    direct = pack(amplitudes, listed, False)
    direct = lax.all_to_all(direct, "owner", 0, 0, tiled=True)
    before = lax.ppermute(quarter, "task", shift_task(1))
    after = lax.ppermute(quarter, "task", shift_task(-1))
    across = [
        lax.ppermute(before[: OWNERS // 2], "task", shift_task(1)),
        lax.ppermute(after[OWNERS // 2 :], "task", shift_task(-1)),
    ]

    def whole_slots(t):
        return t % TASKS * WHOLE + jnp.arange(WHOLE)

    def half_slots(*tasks):
        tasks = jnp.stack(tasks) % TASKS
        return TASKS * WHOLE + tasks // HALVES, tasks % HALVES

    near_ids, near_half = half_slots(task, task - 1)
    late_ids, late_half = half_slots(task + 1, task + 2)
    near_slots = [whole_slots(task), whole_slots(task - 1), whole_slots(task + 1), near_ids]
    late_slots = [jnp.arange(SHARED, live), whole_slots(task + 2), late_ids]
    slots = jnp.take(mine, jnp.concatenate(near_slots + late_slots))
    cut = 3 * WHOLE + HALVES
    near_slots, late_slots = slots[:cut], slots[cut:]

    def units(sources, j):
        return [(p, HALVES * j + h, k, len(sources), h) for k, p in enumerate(sources) for h in range(HALVES)]

    last = UNITS - 1
    near_plan = [units([p], j) for p in range(3) for j in range(WHOLE)] + [[(0, last, 0, 1, 0), (1, last, 0, 1, 1)]]
    late_plan = [[(0, j, 0, 1, None)] for j in range(live - SHARED)] + [units([2, 3], j) for j in range(WHOLE)]
    late_plan.append([(1, last, 0, 1, 0), (2, last, 0, 2, 1), (3, last, 1, 2, 1)])

    def places(core):
        dy = (jnp.repeat(jnp.arange(SIDE), SIDE) - y) % SIDE
        dz = (jnp.tile(jnp.arange(SIDE), SIDE) - z) % SIDE
        first, second = jnp.where(core == 0, dz, dy), jnp.where(core == 0, dy, dz)
        return (first % 2 * 2 + first // 2) * SIDE + second

    cores = jnp.stack([1 - c, c])
    where_to = jnp.concatenate([places(1 - c), places(c)])
    both = product(
        [quarter, before, after], near_plan, integrals, near_slots, near_half, cores, where_to, spare=4, name="product_near"
    )
    parts = product(
        [direct, after, *across],
        late_plan,
        integrals,
        late_slots,
        late_half,
        cores,
        where_to,
        both,
        (SIDE, SIDE, 2 * SIDE),
        8,
        name="product_late",
    )
    theirs, ours = ([x.reshape(-1, SIDE, *x.shape[1:]) for x in parts[i : i + 3]] for i in (0, 3))
    farthest = (ours[1] + trade(theirs[1]))[0]
    theirs[0], theirs[2], farthest = lax.optimization_barrier((theirs[0], theirs[2], farthest))
    total = send(farthest, 2)
    sides = ours[2] + trade(theirs[2])
    staying = (ours[0] + trade(theirs[0]))[0]
    total = staying + total + send(sides[0], 1) + send(sides[1], 3)
    return total[0] + send(total[2], 2, 1) + send(total[1], 1, 1) + send(total[3], 3, 1)


def solution(mesh):
    placed = (P("owner", None, None, None), P(None, "owner", "task", None), P())
    return jax.shard_map(
        per_device, mesh=mesh, in_specs=placed, out_specs=P("owner", "task"), check_vma=False
    )
```

time: 138 us -> 135 us (0.978)
  Pallas kernels: 56.4 us -> 45.8 us
  waiting for transfers between devices: 43.3 us -> 49.7 us
  starting transfers between devices: 30.1 us -> 32.2 us
  other arithmetic: 2.54 us -> 4.37 us
  local copies, waits for them, and re-layouts: 4.29 us -> 2.59 us
    pallas_call x6 -> x4, Pallas kernels: 56.4 us -> 45.8 us  [the longest x2 28.9 us: product(): pl.pallas_call(functools.partial(product_kernel, len(pieces), plan, sides...]
    ppermute x1, waiting for transfers between devices: 15.1 us -> 20.4 us  [per_device(): before = lax.ppermute(quarter, 'task', shift_task(1))]
    all_to_all x1, waiting for transfers between devices: 3.85 us -> 0.01 us  [per_device(): direct = lax.all_to_all(direct, 'owner', 0, 0, tiled=True)]
    all_to_all x1, waiting for transfers between devices: 1.74 us -> 5.51 us  [per_device(): quarter = lax.all_to_all(shared, 'owner', 0, 0, tiled=True)]
    ppermute x3 -> x5, waiting for transfers between devices: 0.01 us -> 3.35 us  [the longest x3 3.35 us: trade(): return lax.ppermute(x, 'owner', owner_perm(lambda y, z, c: (y, z, 1 - c)))]
    ppermute x6, starting transfers between devices: 8.97 us -> 11.6 us  [send(): return lax.ppermute(x, 'owner', along(step, swapped))]
    ppermute x6, waiting for transfers between devices: 22.6 us -> 20.4 us  [send(): return lax.ppermute(x, 'owner', along(step, swapped))]
    ppermute x3 -> x5, starting transfers between devices: 3.64 us -> 4.05 us  [the longest x1 3.02 us: per_device(): lax.ppermute(after[OWNERS // 2:], 'task', shift_task(-1))]
  transfers between devices with their start and end apart: 13 -> 15, of which waited for: 8 -> 10; matrix products, arithmetic and copies ran while one was open for 3% -> 3% of each run, Pallas kernels for 29% -> 16%
where the time goes in v2:
time: 135 us
  waiting for transfers between devices  49.7 us (37%)
  Pallas kernels  45.8 us (34%)
  starting transfers between devices  32.2 us (24%)
  other arithmetic  4.37 us (3%)
  local copies, waits for them, and re-layouts  2.59 us (2%)
    pallas_call x2, Pallas kernels, product(): pl.pallas_call(functools.partial(product_kernel, len(pieces), plan, sides...  28.9 us
    ppermute x6, waiting for transfers between devices, send(): return lax.ppermute(x, 'owner', along(step, swapped))  20.4 us
    ppermute x1, waiting for transfers between devices, per_device(): before = lax.ppermute(quarter, 'task', shift_task(1))  20.4 us
    pallas_call x2, Pallas kernels, pack(): pl.pallas_call(functools.partial(pack_kernel, by_task), in_specs=[anywher...  16.9 us
    ppermute x6, starting transfers between devices, send(): return lax.ppermute(x, 'owner', along(step, swapped))  11.6 us
    all_to_all x1, starting transfers between devices, per_device(): quarter = lax.all_to_all(shared, 'owner', 0, 0, tiled=True)  8.43 us
    all_to_all x1, waiting for transfers between devices, per_device(): quarter = lax.all_to_all(shared, 'owner', 0, 0, tiled=True)  5.51 us
    all_to_all x1, starting transfers between devices, per_device(): direct = lax.all_to_all(direct, 'owner', 0, 0, tiled=True)  4.82 us
  transfers between devices with their start and end apart: 15, of which 10 were waited for; matrix products, arithmetic and copies ran while one was open for 3% of the time, Pallas kernels for 16%

profile of v2, /device:TPU:0, one launch (start us, length us, event | category | flops | bytes accessed | tf_op | source)
XLA Modules:
  0.0 135.0 jit_solution(15599115443770889741)
XLA Ops:
  0.0 6.4 %pack_shared.1 = bf16[32,5,24,128]{3,2,1,0:T(8,128)(2,1)} custom-call(s32[18,32]{1,0:T(8,128)} %bitcast.74, bf16[24,20,32,256]{3,2,1,0:T(8,128)(2,1)} %amp_ref.3), custom_call_target="tpu_custom_call" | custom-call | flops 3019898880 | bytes 7864320 | tf_op jit(solution)/shard_map/pack_shared/pallas_call | solution.py:91
  6.4 8.4 %all-to-all-start.1 = ((bf16[32,5,24,128]{3,2,1,0:T(8,128)(2,1)}), bf16[32,5,24,128]{3,2,1,0:T(8,128)(2,1)S(1)}, u32[]{:S(2)}, u32[]{:S(2)}) async-start(bf16[32,5,24,128]{3,2,1,0:T(8,128)(2,1)} %pack_shared.1), calls=%async_computation.1 | async-start | bytes 1966080 | tf_op jit(solution)/shard_map/all_to_all | solution.py:279
  14.9 10.5 %pack_direct.1 = bf16[32,8,24,256]{3,2,1,0:T(8,128)(2,1)} custom-call(s32[18,32]{1,0:T(8,128)} %bitcast.75, bf16[24,20,32,256]{3,2,1,0:T(8,128)(2,1)} %amp_ref.3), custom_call_target="tpu_custom_call" | custom-call | flops 4831838208 | bytes 7864320 | tf_op jit(solution)/shard_map/pack_direct/pallas_call | solution.py:91
  25.4 5.5 %all-to-all-done.1 = bf16[32,5,24,128]{3,2,1,0:T(8,128)(2,1)S(1)} async-done(((bf16[32,5,24,128]{3,2,1,0:T(8,128)(2,1)}), bf16[32,5,24,128]{3,2,1,0:T(8,128)(2,1)S(1)}, u32[]{:S(2)}, u32[]{:S(2)}) %all-to-all-start.1) | async-done | bytes 983072 | tf_op jit(solution)/shard_map/all_to_all | solution.py:279
  30.9 4.8 %all-to-all-start = ((bf16[32,8,24,256]{3,2,1,0:T(8,128)(2,1)}), bf16[32,8,24,256]{3,2,1,0:T(8,128)(2,1)}, u32[]{:S(2)}, u32[]{:S(2)}) async-start(bf16[32,8,24,256]{3,2,1,0:T(8,128)(2,1)} %pack_direct.1), calls=%async_computation | async-start | bytes 6291456 | tf_op jit(solution)/shard_map/all_to_all | solution.py:281
  35.9 0.1 sub.58
  35.9 0.1 sub.62
  36.0 0.1 and_select_fusion.7
  36.1 0.6 and_select_fusion
  36.8 0.1 concatenate.75
  36.9 0.2 dynamic-slice_reduce_fusion
  37.1 0.7 gather_fusion
  37.8 1.6 %collective-permute-start.1 = (bf16[32,5,24,128]{3,2,1,0:T(8,128)(2,1)S(1)}, bf16[32,5,24,128]{3,2,1,0:T(8,128)(2,1)S(1)}, u32[]{:S(2)}, u32[]{:S(2)}) collective-permute-start(bf16[32,5,24,128]{3,2,1,0:T(8,128)(2,1)S(1)} %all-to-all-done.1), channel_id=1, source_target_pairs={{0,1},{1,2},{2,3},{3,0},{4,5},{5,6},{6,7},{7,4},{8,9},{9,10},{10,1... | collective-permute-start | bytes 2949128 | tf_op jit(solution)/shard_map/ppermute | solution.py:282
  39.4 1.7 %collective-permute-start = (bf16[32,5,24,128]{3,2,1,0:T(8,128)(2,1)S(1)}, bf16[32,5,24,128]{3,2,1,0:T(8,128)(2,1)S(1)}, u32[]{:S(2)}, u32[]{:S(2)}) collective-permute-start(bf16[32,5,24,128]{3,2,1,0:T(8,128)(2,1)S(1)} %all-to-all-done.1), channel_id=1, source_target_pairs={{0,3},{1,0},{2,1},{3,2},{4,7},{5,4},{6,5},{7,6},{8,11},{9,8},{10,9... | collective-permute-start | bytes 2949128 | tf_op jit(solution)/shard_map/ppermute | solution.py:283
  41.1 0.1 concatenate.67
  41.2 0.1 slice.30.slots_ref
  41.3 0.6 pad_add_fusion.core_ref
  41.9 0.6 pad_add_fusion.1.places_ref
  42.5 20.4 %collective-permute-done.1 = bf16[32,5,24,128]{3,2,1,0:T(8,128)(2,1)S(1)} collective-permute-done((bf16[32,5,24,128]{3,2,1,0:T(8,128)(2,1)S(1)}, bf16[32,5,24,128]{3,2,1,0:T(8,128)(2,1)S(1)}, u32[]{:S(2)}, u32[]{:S(2)}) %collective-permute-start.1) | collective-permute-done | bytes 983072 | tf_op jit(solution)/shard_map/ppermute | solution.py:282
  62.9 1.0 copy-done.4
  63.9 0.1 slice.42
  63.9 0.3 collective-permute-start.2
  64.3 0.1 slice.43
  64.3 3.0 %collective-permute-start.3 = (bf16[16,5,24,128]{3,2,1,0:T(8,128)(2,1)S(1)}, bf16[16,5,24,128]{3,2,1,0:T(8,128)(2,1)S(1)}, u32[]{:S(2)}, u32[]{:S(2)}) collective-permute-start(bf16[16,5,24,128]{3,2,1,0:T(8,128)(2,1)S(1)} %slice.43), channel_id=1, source_target_pairs={{0,3},{1,0},{2,1},{3,2},{4,7},{5,4},{6,5},{7,6},{8,11},{9,8},{10,9... | collective-permute-start | bytes 1474568 | tf_op jit(solution)/shard_map/ppermute | solution.py:286
  67.4 11.5 %product_near.1 = (f32[16,24,2048]{2,1,0:T(8,128)}, f32[16,24,2048]{2,1,0:T(8,128)}) custom-call(s32[8]{0:T(128)} %bitcast.78, s32[2]{0:T(128)} %get-tuple-element.27.half_ref, s32[2]{0:T(128)} %pad_add_fusion.core_ref, s32[32]{0:T(128)} %pad_add_fusion.1.places_ref, bf16[16,2,5,24,128]{4,3,2,1,0:T(8,128)(2,1)} %bitcast.69, ...), custom_call_target="tpu_custom_call" | custom-call | flops 5637144576 | bytes 13631488 | tf_op jit(solution)/shard_map/product_near/pallas_call | solution.py:236
  79.0 17.3 %product_late.1 = (f32[4,24,2048]{2,1,0:T(8,128)S(1)}, f32[4,24,2048]{2,1,0:T(8,128)}, f32[8,24,2048]{2,1,0:T(8,128)}, f32[4,24,2048]{2,1,0:T(8,128)}, f32[4,24,2048]{2,1,0:T(8,128)}, /*index=5*/f32[8,24,2048]{2,1,0:T(8,128)}) custom-call(s32[12]{0:T(128)S(1)} %slice.30.slots_ref, s32[2]{0:T(128)S(1)} %get-tuple-element.32.half_ref, s32[2]{0:T(128)S(1)} %copy-done, ...), custom_call_target="tpu_custom_call" | custom-call | flops 8858370048 | bytes 17825792 | tf_op jit(solution)/shard_map/product_late/pallas_call | solution.py:236
  96.3 0.1 collective-permute-start.4
  96.4 2.5 %collective-permute-done.4 = f32[1,4,24,2048]{3,2,1,0:T(8,128)S(1)} collective-permute-done((f32[1,4,24,2048]{3,2,1,0:T(8,128)}, f32[1,4,24,2048]{3,2,1,0:T(8,128)S(1)}, u32[]{:S(2)}, u32[]{:S(2)}) %collective-permute-start.4) | collective-permute-done | bytes 786464 | tf_op jit(solution)/shard_map/ppermute | solution.py:265
  98.9 1.2 fusion.2
  100.1 0.2 collective-permute-start.7
  100.3 0.4 collective-permute-start.5
  100.7 3.1 %collective-permute-start.6 = (f32[4,24,2048]{2,1,0:T(8,128)S(1)}, f32[4,24,2048]{2,1,0:T(8,128)S(1)}, u32[]{:S(2)}, u32[]{:S(2)}) collective-permute-start(f32[4,24,2048]{2,1,0:T(8,128)S(1)} %fusion.2), channel_id=1, source_target_pairs={{0,16},{4,68},{8,24},{12,76},{16,0},{20,84},{24,8},{28,92},{32,48}... | collective-permute-start | bytes 2359304 | tf_op jit(solution)/shard_map/ppermute | solution.py:261
  103.8 0.9 collective-permute-done.7
  104.7 0.2 add.336
  104.9 0.1 slice_bitcast_fusion.1
  105.1 1.7 %collective-permute-start.8 = (f32[4,24,2048]{2,1,0:T(8,128)S(1)}, f32[4,24,2048]{2,1,0:T(8,128)S(1)}, u32[]{:S(2)}, u32[]{:S(2)}) collective-permute-start(f32[4,24,2048]{2,1,0:T(8,128)S(1)} %get-tuple-element.34), channel_id=1, source_target_pairs={{0,8},{4,36},{8,16},{12,44},{16,24},{20,52},{24,0},{28,60},{32,40}... | collective-permute-start | bytes 2359304 | tf_op jit(solution)/shard_map/ppermute | solution.py:261
  106.7 1.6 %collective-permute-start.9 = (f32[4,24,2048]{2,1,0:T(8,128)S(1)}, f32[4,24,2048]{2,1,0:T(8,128)S(1)}, u32[]{:S(2)}, u32[]{:S(2)}) collective-permute-start(f32[4,24,2048]{2,1,0:T(8,128)S(1)} %get-tuple-element.35), channel_id=1, source_target_pairs={{0,24},{4,100},{8,0},{12,108},{16,8},{20,116},{24,16},{28,124},{32... | collective-permute-start | bytes 2359304 | tf_op jit(solution)/shard_map/ppermute | solution.py:261
  108.4 5.9 %collective-permute-done.6 = f32[4,24,2048]{2,1,0:T(8,128)S(1)} collective-permute-done((f32[4,24,2048]{2,1,0:T(8,128)S(1)}, f32[4,24,2048]{2,1,0:T(8,128)S(1)}, u32[]{:S(2)}, u32[]{:S(2)}) %collective-permute-start.6) | collective-permute-done | bytes 786464 | tf_op jit(solution)/shard_map/ppermute | solution.py:261
  114.3 8.3 %collective-permute-done.8 = f32[4,24,2048]{2,1,0:T(8,128)S(1)} collective-permute-done((f32[4,24,2048]{2,1,0:T(8,128)S(1)}, f32[4,24,2048]{2,1,0:T(8,128)S(1)}, u32[]{:S(2)}, u32[]{:S(2)}) %collective-permute-start.8) | collective-permute-done | bytes 786464 | tf_op jit(solution)/shard_map/ppermute | solution.py:261
  122.6 0.2 collective-permute-done.9
  122.8 0.2 fusion.1
  123.1 3.2 %collective-permute-start.10 = (f32[24,2048]{1,0:T(8,128)S(1)}, f32[24,2048]{1,0:T(8,128)S(1)}, u32[]{:S(2)}, u32[]{:S(2)}) collective-permute-start(f32[24,2048]{1,0:T(8,128)S(1)} %get-tuple-element.36), channel_id=1, source_target_pairs={{0,64},{4,20},{8,72},{12,28},{16,80},{20,4},{24,88},{28,12},{32,96... | collective-permute-start | bytes 589832 | tf_op jit(solution)/shard_map/ppermute | solution.py:261
  126.3 1.1 collective-permute-start.12
  127.4 0.9 collective-permute-start.11
  128.3 2.1 %collective-permute-done.10 = f32[24,2048]{1,0:T(8,128)S(1)} collective-permute-done((f32[24,2048]{1,0:T(8,128)S(1)}, f32[24,2048]{1,0:T(8,128)S(1)}, u32[]{:S(2)}, u32[]{:S(2)}) %collective-permute-start.10) | collective-permute-done | bytes 196640 | tf_op jit(solution)/shard_map/ppermute | solution.py:261
  130.4 2.3 %collective-permute-done.12 = f32[24,2048]{1,0:T(8,128)S(1)} collective-permute-done((f32[24,2048]{1,0:T(8,128)S(1)}, f32[24,2048]{1,0:T(8,128)S(1)}, u32[]{:S(2)}, u32[]{:S(2)}) %collective-permute-start.12) | collective-permute-done | bytes 196640 | tf_op jit(solution)/shard_map/ppermute | solution.py:261
  132.7 1.6 %collective-permute-done.11 = f32[24,2048]{1,0:T(8,128)S(1)} collective-permute-done((f32[24,2048]{1,0:T(8,128)S(1)}, f32[24,2048]{1,0:T(8,128)S(1)}, u32[]{:S(2)}, u32[]{:S(2)}) %collective-permute-start.11) | collective-permute-done | bytes 196640 | tf_op jit(solution)/shard_map/ppermute | solution.py:261
  134.3 0.7 fusion.5
  (37 shorter events, 0.2 us)
Async XLA Ops:
  6.4 24.5 %all-to-all-start.1 = ((bf16[32,5,24,128]{3,2,1,0:T(8,128)(2,1)}), bf16[32,5,24,128]{3,2,1,0:T(8,128)(2,1)S(1)}, u32[]{:S(2)}, u32[]{:S(2)}) async-start(bf16[32,5,24,128]{3,2,1,0:T(8,128)(2,1)} %pack_shared.1), calls=%async_computation.1 | async-start | bytes 1966080 | tf_op jit(solution)/shard_map/all_to_all | solution.py:279
  25.4 11.5 %copy-start.7 = (s32[32,18]{0,1:T(8,128)S(1)}, s32[32,18]{0,1:T(8,128)}, u32[]{:S(2)}) copy-start(s32[32,18]{0,1:T(8,128)} %param.5) | copy-start | bytes 6916
  30.9 8.4 %copy-start.2 = (bf16[32,5,24,128]{3,2,1,0:T(8,128)(2,1)}, bf16[32,5,24,128]{3,2,1,0:T(8,128)(2,1)S(1)}, u32[]{:S(2)}) copy-start(bf16[32,5,24,128]{3,2,1,0:T(8,128)(2,1)S(1)} %all-to-all-done.1) | copy-start | bytes 2949124
  30.9 48.0 %all-to-all-start = ((bf16[32,8,24,256]{3,2,1,0:T(8,128)(2,1)}), bf16[32,8,24,256]{3,2,1,0:T(8,128)(2,1)}, u32[]{:S(2)}, u32[]{:S(2)}) async-start(bf16[32,8,24,256]{3,2,1,0:T(8,128)(2,1)} %pack_direct.1), calls=%async_computation | async-start | bytes 6291456 | tf_op jit(solution)/shard_map/all_to_all | solution.py:281
  37.8 25.1 %collective-permute-start.1 = (bf16[32,5,24,128]{3,2,1,0:T(8,128)(2,1)S(1)}, bf16[32,5,24,128]{3,2,1,0:T(8,128)(2,1)S(1)}, u32[]{:S(2)}, u32[]{:S(2)}) collective-permute-start(bf16[32,5,24,128]{3,2,1,0:T(8,128)(2,1)S(1)} %all-to-all-done.1), channel_id=1, source_target_pairs={{0,1},{1,2},{2,3},{3,0},{4,5},{5,6},{6,7},{7,4},{8,9},{9,10},{10,1... | collective-permute-start | bytes 2949128 | tf_op jit(solution)/shard_map/ppermute | solution.py:282
  39.4 24.9 %collective-permute-start = (bf16[32,5,24,128]{3,2,1,0:T(8,128)(2,1)S(1)}, bf16[32,5,24,128]{3,2,1,0:T(8,128)(2,1)S(1)}, u32[]{:S(2)}, u32[]{:S(2)}) collective-permute-start(bf16[32,5,24,128]{3,2,1,0:T(8,128)(2,1)S(1)} %all-to-all-done.1), channel_id=1, source_target_pairs={{0,3},{1,0},{2,1},{3,2},{4,7},{5,4},{6,5},{7,6},{8,11},{9,8},{10,9... | collective-permute-start | bytes 2949128 | tf_op jit(solution)/shard_map/ppermute | solution.py:283
  41.2 26.2 %copy-start.8 = (s32[20]{0:T(128)}, s32[20]{0:T(128)S(1)}, u32[]{:S(2)}) copy-start(s32[20]{0:T(128)S(1)} %and_select_fusion.8) | copy-start | bytes 244
  62.9 1.0 copy-start.4
  63.9 15.0 %collective-permute-start.2 = (bf16[16,5,24,128]{3,2,1,0:T(8,128)(2,1)S(1)}, bf16[16,5,24,128]{3,2,1,0:T(8,128)(2,1)S(1)}, u32[]{:S(2)}, u32[]{:S(2)}) collective-permute-start(bf16[16,5,24,128]{3,2,1,0:T(8,128)(2,1)S(1)} %slice.42), channel_id=1, source_target_pairs={{0,1},{1,2},{2,3},{3,0},{4,5},{5,6},{6,7},{7,4},{8,9},{9,10},{10,1... | collective-permute-start | bytes 1474568 | tf_op jit(solution)/shard_map/ppermute | solution.py:285
  64.3 3.1 %copy-start.3 = (bf16[32,5,24,128]{3,2,1,0:T(8,128)(2,1)}, bf16[32,5,24,128]{3,2,1,0:T(8,128)(2,1)S(1)}, u32[]{:S(2)}) copy-start(bf16[32,5,24,128]{3,2,1,0:T(8,128)(2,1)S(1)} %collective-permute-done) | copy-start | bytes 2949124
  64.3 14.6 %collective-permute-start.3 = (bf16[16,5,24,128]{3,2,1,0:T(8,128)(2,1)S(1)}, bf16[16,5,24,128]{3,2,1,0:T(8,128)(2,1)S(1)}, u32[]{:S(2)}, u32[]{:S(2)}) collective-permute-start(bf16[16,5,24,128]{3,2,1,0:T(8,128)(2,1)S(1)} %slice.43), channel_id=1, source_target_pairs={{0,3},{1,0},{2,1},{3,2},{4,7},{5,4},{6,5},{7,6},{8,11},{9,8},{10,9... | collective-permute-start | bytes 1474568 | tf_op jit(solution)/shard_map/ppermute | solution.py:286
  67.4 11.6 %copy-start = (s32[2]{0:T(128)S(1)}, s32[2]{0:T(128)}, u32[]{:S(2)}) copy-start(s32[2]{0:T(128)} %pad_add_fusion.core_ref) | copy-start | bytes 28
  67.4 11.6 %copy-start.1 = (s32[32]{0:T(128)S(1)}, s32[32]{0:T(128)}, u32[]{:S(2)}) copy-start(s32[32]{0:T(128)} %pad_add_fusion.1.places_ref) | copy-start | bytes 388
  96.3 8.4 %copy-start.5 = (f32[8,24,2048]{2,1,0:T(8,128)S(1)}, f32[8,24,2048]{2,1,0:T(8,128)}, u32[]{:S(2)}) copy-start(f32[8,24,2048]{2,1,0:T(8,128)} %get-tuple-element.25) | copy-start | bytes 4718596
  96.3 2.6 %collective-permute-start.4 = (f32[1,4,24,2048]{3,2,1,0:T(8,128)}, f32[1,4,24,2048]{3,2,1,0:T(8,128)S(1)}, u32[]{:S(2)}, u32[]{:S(2)}) collective-permute-start(f32[1,4,24,2048]{3,2,1,0:T(8,128)} %bitcast.80), channel_id=1, source_target_pairs={{0,4},{4,0},{8,12},{12,8},{16,20},{20,16},{24,28},{28,24},{32,36},... | collective-permute-start | bytes 2359304 | tf_op jit(solution)/shard_map/ppermute | solution.py:265
  100.1 4.6 %collective-permute-start.7 = (f32[2,4,24,2048]{3,2,1,0:T(8,128)}, f32[2,4,24,2048]{3,2,1,0:T(8,128)S(1)}, u32[]{:S(2)}, u32[]{:S(2)}) collective-permute-start(f32[2,4,24,2048]{3,2,1,0:T(8,128)} %bitcast.79), channel_id=1, source_target_pairs={{0,4},{4,0},{8,12},{12,8},{16,20},{20,16},{24,28},{28,24},{32,36},... | collective-permute-start | bytes 4718600 | tf_op jit(solution)/shard_map/ppermute | solution.py:265
  100.3 8.1 %collective-permute-start.5 = (f32[1,4,24,2048]{3,2,1,0:T(8,128)S(1)}, f32[1,4,24,2048]{3,2,1,0:T(8,128)S(1)}, u32[]{:S(2)}, u32[]{:S(2)}) collective-permute-start(f32[1,4,24,2048]{3,2,1,0:T(8,128)S(1)} %bitcast.66), channel_id=1, source_target_pairs={{0,4},{4,0},{8,12},{12,8},{16,20},{20,16},{24,28},{28,24},{32,36},... | collective-permute-start | bytes 2359304 | tf_op jit(solution)/shard_map/ppermute | solution.py:265
  100.7 13.6 %collective-permute-start.6 = (f32[4,24,2048]{2,1,0:T(8,128)S(1)}, f32[4,24,2048]{2,1,0:T(8,128)S(1)}, u32[]{:S(2)}, u32[]{:S(2)}) collective-permute-start(f32[4,24,2048]{2,1,0:T(8,128)S(1)} %fusion.2), channel_id=1, source_target_pairs={{0,16},{4,68},{8,24},{12,76},{16,0},{20,84},{24,8},{28,92},{32,48}... | collective-permute-start | bytes 2359304 | tf_op jit(solution)/shard_map/ppermute | solution.py:261
  104.7 18.1 %copy-start.6 = (f32[4,24,2048]{2,1,0:T(8,128)S(1)}, f32[4,24,2048]{2,1,0:T(8,128)}, u32[]{:S(2)}) copy-start(f32[4,24,2048]{2,1,0:T(8,128)} %get-tuple-element.18) | copy-start | bytes 2359300
  105.1 17.5 %collective-permute-start.8 = (f32[4,24,2048]{2,1,0:T(8,128)S(1)}, f32[4,24,2048]{2,1,0:T(8,128)S(1)}, u32[]{:S(2)}, u32[]{:S(2)}) collective-permute-start(f32[4,24,2048]{2,1,0:T(8,128)S(1)} %get-tuple-element.34), channel_id=1, source_target_pairs={{0,8},{4,36},{8,16},{12,44},{16,24},{20,52},{24,0},{28,60},{32,40}... | collective-permute-start | bytes 2359304 | tf_op jit(solution)/shard_map/ppermute | solution.py:261
  106.7 16.1 %collective-permute-start.9 = (f32[4,24,2048]{2,1,0:T(8,128)S(1)}, f32[4,24,2048]{2,1,0:T(8,128)S(1)}, u32[]{:S(2)}, u32[]{:S(2)}) collective-permute-start(f32[4,24,2048]{2,1,0:T(8,128)S(1)} %get-tuple-element.35), channel_id=1, source_target_pairs={{0,24},{4,100},{8,0},{12,108},{16,8},{20,116},{24,16},{28,124},{32... | collective-permute-start | bytes 2359304 | tf_op jit(solution)/shard_map/ppermute | solution.py:261
  123.1 7.3 %collective-permute-start.10 = (f32[24,2048]{1,0:T(8,128)S(1)}, f32[24,2048]{1,0:T(8,128)S(1)}, u32[]{:S(2)}, u32[]{:S(2)}) collective-permute-start(f32[24,2048]{1,0:T(8,128)S(1)} %get-tuple-element.36), channel_id=1, source_target_pairs={{0,64},{4,20},{8,72},{12,28},{16,80},{20,4},{24,88},{28,12},{32,96... | collective-permute-start | bytes 589832 | tf_op jit(solution)/shard_map/ppermute | solution.py:261
  126.3 6.4 %collective-permute-start.12 = (f32[24,2048]{1,0:T(8,128)S(1)}, f32[24,2048]{1,0:T(8,128)S(1)}, u32[]{:S(2)}, u32[]{:S(2)}) collective-permute-start(f32[24,2048]{1,0:T(8,128)S(1)} %get-tuple-element.37), channel_id=1, source_target_pairs={{0,96},{4,28},{8,104},{12,4},{16,112},{20,12},{24,120},{28,20},{32... | collective-permute-start | bytes 589832 | tf_op jit(solution)/shard_map/ppermute | solution.py:261
  127.4 6.9 %collective-permute-start.11 = (f32[24,2048]{1,0:T(8,128)S(1)}, f32[24,2048]{1,0:T(8,128)S(1)}, u32[]{:S(2)}, u32[]{:S(2)}) collective-permute-start(f32[24,2048]{1,0:T(8,128)S(1)} %get-tuple-element.38), channel_id=1, source_target_pairs={{0,32},{4,12},{8,40},{12,20},{16,48},{20,28},{24,56},{28,4},{32,64... | collective-permute-start | bytes 589832 | tf_op jit(solution)/shard_map/ppermute | solution.py:261

commit v3 on v2

--- a/solution.py
+++ b/solution.py
@@ -43,18 +43,23 @@
     owners, count, pairs, _ = out_ref.shape
     tiles, _, _, ct = source.shape
     task = lax.axis_index("task")
-    copies = [pltpu.make_async_copy(nz_ref, listed, nz_sem)]
-    for k in range(tiles):
-        copies.append(pltpu.make_async_copy(amp_ref.at[:, k], source.at[k], sem.at[k]))
-    for copy in copies:
-        copy.start()
+    half = owners // 2
+
+    def fetch(side, k):
+        here = slice(side * half, (side + 1) * half)
+        return pltpu.make_async_copy(amp_ref.at[:, k, here], source.at[k, :, here], sem.at[side, k])
+
+    listing = pltpu.make_async_copy(nz_ref, listed, nz_sem)
+    listing.start()
+    for side in range(2):
+        for k in range(tiles):
+            fetch(side, k).start()
 
     n = pairs * GROUP
     row = lax.broadcasted_iota(jnp.int32, (n, n), 0)
     column = lax.broadcasted_iota(jnp.int32, (n, n), 1)
     turn = (row == column % GROUP * pairs + column // GROUP).astype(F32).astype(source.dtype)
-    for copy in copies:
-        copy.wait()
+    listing.wait()
 
     def block(o, slot):
         j = o % GROUP
@@ -62,26 +67,31 @@
         product = jnp.dot(turn[j * pairs : (j + 1) * pairs], rows, preferred_element_type=F32)
         return product.astype(out_ref.dtype)
 
-    def give(i, carry):
-        for o in range(owners):
-            out_ref[o, i] = block(o, SHARED + i)
-        return carry
-
-    def give_units(i, carry):
-        for o in range(owners):
-            both = block(o, task * WHOLE + i)
-            for h in range(HALVES):
-                out_ref[o, HALVES * i + h] = both[:, h * LANES : (h + 1) * LANES]
-        return carry
-
-    if not by_task:
-        lax.fori_loop(0, count, give, 0)
-        return
-    lax.fori_loop(0, WHOLE, give_units, 0)
-    for o in range(owners):
-        both = block(o, TASKS * WHOLE + task // HALVES)
-        halves = [both[:, h * LANES : (h + 1) * LANES] for h in range(HALVES)]
-        out_ref[o, UNITS - 1] = jnp.where(task % HALVES == 0, *halves)
+    for side in range(2):
+        for k in range(tiles):
+            fetch(side, k).wait()
+        here = range(side * half, (side + 1) * half)
+
+        def give(i, carry, here=here):
+            for o in here:
+                out_ref[o, i] = block(o, SHARED + i)
+            return carry
+
+        def give_units(i, carry, here=here):
+            for o in here:
+                both = block(o, task * WHOLE + i)
+                for h in range(HALVES):
+                    out_ref[o, HALVES * i + h] = both[:, h * LANES : (h + 1) * LANES]
+            return carry
+
+        if not by_task:
+            lax.fori_loop(0, count, give, 0)
+            continue
+        lax.fori_loop(0, WHOLE, give_units, 0)
+        for o in here:
+            both = block(o, TASKS * WHOLE + task // HALVES)
+            halves = [both[:, h * LANES : (h + 1) * LANES] for h in range(HALVES)]
+            out_ref[o, UNITS - 1] = jnp.where(task % HALVES == 0, *halves)
 
 
 def pack(amplitudes, listed, by_task):
@@ -97,7 +107,7 @@
             pltpu.SMEM(listed.shape, jnp.int32),
             pltpu.VMEM((tiles, pairs, owners, ct), amplitudes.dtype),
             pltpu.SemaphoreType.DMA,
-            pltpu.SemaphoreType.DMA((tiles,)),
+            pltpu.SemaphoreType.DMA((2, tiles)),
         ],
         compiler_params=pltpu.CompilerParams(vmem_limit_bytes=60 << 20),
         cost_estimate=pl.CostEstimate(
@@ -318,7 +328,7 @@
     cores = jnp.stack([1 - c, c])
     where_to = jnp.concatenate([places(1 - c), places(c)])
     both = product(
-        [quarter, before, after], near_plan, integrals, near_slots, near_half, cores, where_to, spare=4, name="product_near"
+        [quarter, before, after], near_plan, integrals, near_slots, near_half, cores, where_to, spare=5, name="product_near"
     )
     parts = product(
         [direct, after, *across],
@@ -330,7 +340,7 @@
         where_to,
         both,
         (SIDE, SIDE, 2 * SIDE),
-        8,
+        14,
         name="product_late",
     )
     theirs, ours = ([x.reshape(-1, SIDE, *x.shape[1:]) for x in parts[i : i + 3]] for i in (0, 3))

time: 135 us -> 135 us (level)
  transfers between devices with their start and end apart: 15 -> 15, of which waited for: 10 -> 9; matrix products, arithmetic and copies ran while one was open for 3% -> 3% of each run, Pallas kernels for 16% -> 17%
where the time goes in v3:
time: 135 us; the launch traced here: 134 us
  waiting for transfers between devices  49.4 us (37%)
  Pallas kernels  45.1 us (33%)
  starting transfers between devices  32.4 us (24%)
  local copies, waits for them, and re-layouts  3.72 us (3%)
  other arithmetic  3.36 us (2%)
    pallas_call x2, Pallas kernels, product(): pl.pallas_call(functools.partial(product_kernel, len(pieces), plan, sides...  28.5 us
    ppermute x6, waiting for transfers between devices, send(): return lax.ppermute(x, 'owner', along(step, swapped))  21.4 us
    ppermute x1, waiting for transfers between devices, per_device(): before = lax.ppermute(quarter, 'task', shift_task(1))  20.4 us
    pallas_call x2, Pallas kernels, pack(): pl.pallas_call(functools.partial(pack_kernel, by_task), in_specs=[anywher...  16.7 us
    ppermute x6, starting transfers between devices, send(): return lax.ppermute(x, 'owner', along(step, swapped))  11.6 us
    all_to_all x1, starting transfers between devices, per_device(): quarter = lax.all_to_all(shared, 'owner', 0, 0, tiled=True)  8.43 us
    all_to_all x1, waiting for transfers between devices, per_device(): quarter = lax.all_to_all(shared, 'owner', 0, 0, tiled=True)  5.32 us
    all_to_all x1, starting transfers between devices, per_device(): direct = lax.all_to_all(direct, 'owner', 0, 0, tiled=True)  4.82 us
  transfers between devices with their start and end apart: 15, of which 9 were waited for; matrix products, arithmetic and copies ran while one was open for 3% of the time, Pallas kernels for 17%

profile of v3, /device:TPU:0, one launch (start us, length us, event | category | flops | bytes accessed | tf_op | source)
XLA Modules:
  0.0 134.3 jit_solution(404238092342365529)
XLA Ops:
  0.0 6.0 %pack_shared.1 = bf16[32,5,24,128]{3,2,1,0:T(8,128)(2,1)} custom-call(s32[18,32]{1,0:T(8,128)} %bitcast.76, bf16[24,20,32,256]{3,2,1,0:T(8,128)(2,1)} %amp_ref.3), custom_call_target="tpu_custom_call" | custom-call | flops 3019898880 | bytes 7864320 | tf_op jit(solution)/shard_map/pack_shared/pallas_call | solution.py:101
  6.0 8.4 %all-to-all-start.1 = ((bf16[32,5,24,128]{3,2,1,0:T(8,128)(2,1)}), bf16[32,5,24,128]{3,2,1,0:T(8,128)(2,1)S(1)}, u32[]{:S(2)}, u32[]{:S(2)}) async-start(bf16[32,5,24,128]{3,2,1,0:T(8,128)(2,1)} %pack_shared.1), calls=%async_computation.1 | async-start | bytes 1966080 | tf_op jit(solution)/shard_map/all_to_all | solution.py:289
  14.4 10.7 %pack_direct.1 = bf16[32,8,24,256]{3,2,1,0:T(8,128)(2,1)} custom-call(s32[18,32]{1,0:T(8,128)} %bitcast.77, bf16[24,20,32,256]{3,2,1,0:T(8,128)(2,1)} %amp_ref.3), custom_call_target="tpu_custom_call" | custom-call | flops 4831838208 | bytes 7864320 | tf_op jit(solution)/shard_map/pack_direct/pallas_call | solution.py:101
  25.2 5.3 %all-to-all-done.1 = bf16[32,5,24,128]{3,2,1,0:T(8,128)(2,1)S(1)} async-done(((bf16[32,5,24,128]{3,2,1,0:T(8,128)(2,1)}), bf16[32,5,24,128]{3,2,1,0:T(8,128)(2,1)S(1)}, u32[]{:S(2)}, u32[]{:S(2)}) %all-to-all-start.1) | async-done | bytes 983072 | tf_op jit(solution)/shard_map/all_to_all | solution.py:289
  30.5 4.8 %all-to-all-start = ((bf16[32,8,24,256]{3,2,1,0:T(8,128)(2,1)}), bf16[32,8,24,256]{3,2,1,0:T(8,128)(2,1)}, u32[]{:S(2)}, u32[]{:S(2)}) async-start(bf16[32,8,24,256]{3,2,1,0:T(8,128)(2,1)} %pack_direct.1), calls=%async_computation | async-start | bytes 6291456 | tf_op jit(solution)/shard_map/all_to_all | solution.py:291
  35.4 0.1 sub.58
  35.5 0.1 sub.62
  35.6 0.1 and_select_fusion.7
  35.7 0.7 and_select_fusion
  36.4 0.1 concatenate.75
  36.5 0.2 dynamic-slice_reduce_fusion
  36.7 0.7 gather_fusion
  37.4 1.6 %collective-permute-start.1 = (bf16[32,5,24,128]{3,2,1,0:T(8,128)(2,1)S(1)}, bf16[32,5,24,128]{3,2,1,0:T(8,128)(2,1)S(1)}, u32[]{:S(2)}, u32[]{:S(2)}) collective-permute-start(bf16[32,5,24,128]{3,2,1,0:T(8,128)(2,1)S(1)} %all-to-all-done.1), channel_id=1, source_target_pairs={{0,1},{1,2},{2,3},{3,0},{4,5},{5,6},{6,7},{7,4},{8,9},{9,10},{10,1... | collective-permute-start | bytes 2949128 | tf_op jit(solution)/shard_map/ppermute | solution.py:292
  39.0 1.7 %collective-permute-start = (bf16[32,5,24,128]{3,2,1,0:T(8,128)(2,1)S(1)}, bf16[32,5,24,128]{3,2,1,0:T(8,128)(2,1)S(1)}, u32[]{:S(2)}, u32[]{:S(2)}) collective-permute-start(bf16[32,5,24,128]{3,2,1,0:T(8,128)(2,1)S(1)} %all-to-all-done.1), channel_id=1, source_target_pairs={{0,3},{1,0},{2,1},{3,2},{4,7},{5,4},{6,5},{7,6},{8,11},{9,8},{10,9... | collective-permute-start | bytes 2949128 | tf_op jit(solution)/shard_map/ppermute | solution.py:293
  40.7 0.1 concatenate.67
  40.8 0.1 slice.30.slots_ref
  40.9 0.6 pad_add_fusion.core_ref
  41.5 0.6 pad_add_fusion.1.places_ref
  42.1 20.4 %collective-permute-done.1 = bf16[32,5,24,128]{3,2,1,0:T(8,128)(2,1)S(1)} collective-permute-done((bf16[32,5,24,128]{3,2,1,0:T(8,128)(2,1)S(1)}, bf16[32,5,24,128]{3,2,1,0:T(8,128)(2,1)S(1)}, u32[]{:S(2)}, u32[]{:S(2)}) %collective-permute-start.1) | collective-permute-done | bytes 983072 | tf_op jit(solution)/shard_map/ppermute | solution.py:292
  62.5 1.0 copy-done.5
  63.5 0.1 slice.42
  63.5 0.3 collective-permute-start.2
  63.9 0.1 slice.43
  63.9 3.0 %collective-permute-start.3 = (bf16[16,5,24,128]{3,2,1,0:T(8,128)(2,1)S(1)}, bf16[16,5,24,128]{3,2,1,0:T(8,128)(2,1)S(1)}, u32[]{:S(2)}, u32[]{:S(2)}) collective-permute-start(bf16[16,5,24,128]{3,2,1,0:T(8,128)(2,1)S(1)} %slice.43), channel_id=1, source_target_pairs={{0,3},{1,0},{2,1},{3,2},{4,7},{5,4},{6,5},{7,6},{8,11},{9,8},{10,9... | collective-permute-start | bytes 1474568 | tf_op jit(solution)/shard_map/ppermute | solution.py:296
  67.0 11.5 %product_near.1 = (f32[16,24,2048]{2,1,0:T(8,128)}, f32[16,24,2048]{2,1,0:T(8,128)}) custom-call(s32[8]{0:T(128)} %bitcast.80, s32[2]{0:T(128)} %get-tuple-element.27.half_ref, s32[2]{0:T(128)} %pad_add_fusion.core_ref, s32[32]{0:T(128)} %pad_add_fusion.1.places_ref, bf16[16,2,5,24,128]{4,3,2,1,0:T(8,128)(2,1)} %bitcast.74, ...), custom_call_target="tpu_custom_call" | custom-call | flops 5637144576 | bytes 13631488 | tf_op jit(solution)/shard_map/product_near/pallas_call | solution.py:246
  78.6 1.2 copy-done.1
  79.8 16.9 %product_late.1 = (f32[4,24,2048]{2,1,0:T(8,128)S(1)}, f32[4,24,2048]{2,1,0:T(8,128)S(1)}, f32[8,24,2048]{2,1,0:T(8,128)S(1)}, f32[4,24,2048]{2,1,0:T(8,128)S(1)...) custom-call(s32[12]{0:T(128)S(1)} %slice.30.slots_ref, s32[2]{0:T(128)S(1)} %get-tuple-element.32.half_ref, ...), custom_call_target="tpu_custom_call" | custom-call | flops 8858370048 | bytes 17825792 | tf_op jit(solution)/shard_map/product_late/pallas_call | solution.py:246
  96.7 0.3 collective-permute-start.4
  97.0 2.3 %collective-permute-done.4 = f32[1,4,24,2048]{3,2,1,0:T(8,128)S(1)} collective-permute-done((f32[1,4,24,2048]{3,2,1,0:T(8,128)S(1)}, f32[1,4,24,2048]{3,2,1,0:T(8,128)S(1)}, u32[]{:S(2)}, u32[]{:S(2)}) %collective-permute-start.4) | collective-permute-done | bytes 786464 | tf_op jit(solution)/shard_map/ppermute | solution.py:275
  99.3 0.1 fusion.2
  99.4 0.2 collective-permute-start.7
  99.6 0.4 collective-permute-start.5
  100.0 3.1 %collective-permute-start.6 = (f32[4,24,2048]{2,1,0:T(8,128)S(1)}, f32[4,24,2048]{2,1,0:T(8,128)S(1)}, u32[]{:S(2)}, u32[]{:S(2)}) collective-permute-start(f32[4,24,2048]{2,1,0:T(8,128)S(1)} %fusion.2), channel_id=1, source_target_pairs={{0,16},{4,68},{8,24},{12,76},{16,0},{20,84},{24,8},{28,92},{32,48}... | collective-permute-start | bytes 2359304 | tf_op jit(solution)/shard_map/ppermute | solution.py:271
  103.1 0.2 add.336
  103.3 0.1 slice_bitcast_fusion.1
  103.4 1.4 %collective-permute-start.8 = (f32[4,24,2048]{2,1,0:T(8,128)S(1)}, f32[4,24,2048]{2,1,0:T(8,128)S(1)}, u32[]{:S(2)}, u32[]{:S(2)}) collective-permute-start(f32[4,24,2048]{2,1,0:T(8,128)S(1)} %get-tuple-element.34), channel_id=1, source_target_pairs={{0,8},{4,36},{8,16},{12,44},{16,24},{20,52},{24,0},{28,60},{32,40}... | collective-permute-start | bytes 2359304 | tf_op jit(solution)/shard_map/ppermute | solution.py:271
  104.9 1.9 %collective-permute-start.9 = (f32[4,24,2048]{2,1,0:T(8,128)S(1)}, f32[4,24,2048]{2,1,0:T(8,128)S(1)}, u32[]{:S(2)}, u32[]{:S(2)}) collective-permute-start(f32[4,24,2048]{2,1,0:T(8,128)S(1)} %get-tuple-element.35), channel_id=1, source_target_pairs={{0,24},{4,100},{8,0},{12,108},{16,8},{20,116},{24,16},{28,124},{32... | collective-permute-start | bytes 2359304 | tf_op jit(solution)/shard_map/ppermute | solution.py:271
  106.7 6.8 %collective-permute-done.6 = f32[4,24,2048]{2,1,0:T(8,128)S(1)} collective-permute-done((f32[4,24,2048]{2,1,0:T(8,128)S(1)}, f32[4,24,2048]{2,1,0:T(8,128)S(1)}, u32[]{:S(2)}, u32[]{:S(2)}) %collective-permute-start.6) | collective-permute-done | bytes 786464 | tf_op jit(solution)/shard_map/ppermute | solution.py:271
  113.6 8.3 %collective-permute-done.8 = f32[4,24,2048]{2,1,0:T(8,128)S(1)} collective-permute-done((f32[4,24,2048]{2,1,0:T(8,128)S(1)}, f32[4,24,2048]{2,1,0:T(8,128)S(1)}, u32[]{:S(2)}, u32[]{:S(2)}) %collective-permute-start.8) | collective-permute-done | bytes 786464 | tf_op jit(solution)/shard_map/ppermute | solution.py:271
  121.9 0.2 collective-permute-done.9
  122.1 0.3 fusion.1
  122.4 3.1 %collective-permute-start.10 = (f32[24,2048]{1,0:T(8,128)S(1)}, f32[24,2048]{1,0:T(8,128)S(1)}, u32[]{:S(2)}, u32[]{:S(2)}) collective-permute-start(f32[24,2048]{1,0:T(8,128)S(1)} %get-tuple-element.36), channel_id=1, source_target_pairs={{0,64},{4,20},{8,72},{12,28},{16,80},{20,4},{24,88},{28,12},{32,96... | collective-permute-start | bytes 589832 | tf_op jit(solution)/shard_map/ppermute | solution.py:271
  125.6 1.1 collective-permute-start.12
  126.7 0.9 collective-permute-start.11
  127.6 2.1 %collective-permute-done.10 = f32[24,2048]{1,0:T(8,128)S(1)} collective-permute-done((f32[24,2048]{1,0:T(8,128)S(1)}, f32[24,2048]{1,0:T(8,128)S(1)}, u32[]{:S(2)}, u32[]{:S(2)}) %collective-permute-start.10) | collective-permute-done | bytes 196640 | tf_op jit(solution)/shard_map/ppermute | solution.py:271
  129.7 2.3 %collective-permute-done.12 = f32[24,2048]{1,0:T(8,128)S(1)} collective-permute-done((f32[24,2048]{1,0:T(8,128)S(1)}, f32[24,2048]{1,0:T(8,128)S(1)}, u32[]{:S(2)}, u32[]{:S(2)}) %collective-permute-start.12) | collective-permute-done | bytes 196640 | tf_op jit(solution)/shard_map/ppermute | solution.py:271
  131.9 1.6 %collective-permute-done.11 = f32[24,2048]{1,0:T(8,128)S(1)} collective-permute-done((f32[24,2048]{1,0:T(8,128)S(1)}, f32[24,2048]{1,0:T(8,128)S(1)}, u32[]{:S(2)}, u32[]{:S(2)}) %collective-permute-start.11) | collective-permute-done | bytes 196640 | tf_op jit(solution)/shard_map/ppermute | solution.py:271
  133.6 0.7 fusion.5
  (35 shorter events, 0.2 us)
Async XLA Ops:
  6.0 24.5 %all-to-all-start.1 = ((bf16[32,5,24,128]{3,2,1,0:T(8,128)(2,1)}), bf16[32,5,24,128]{3,2,1,0:T(8,128)(2,1)S(1)}, u32[]{:S(2)}, u32[]{:S(2)}) async-start(bf16[32,5,24,128]{3,2,1,0:T(8,128)(2,1)} %pack_shared.1), calls=%async_computation.1 | async-start | bytes 1966080 | tf_op jit(solution)/shard_map/all_to_all | solution.py:289
  25.2 11.3 %copy-start.6 = (s32[32,18]{0,1:T(8,128)S(1)}, s32[32,18]{0,1:T(8,128)}, u32[]{:S(2)}) copy-start(s32[32,18]{0,1:T(8,128)} %param.5) | copy-start | bytes 6916
  30.5 8.5 %copy-start.4 = (bf16[32,5,24,128]{3,2,1,0:T(8,128)(2,1)}, bf16[32,5,24,128]{3,2,1,0:T(8,128)(2,1)S(1)}, u32[]{:S(2)}) copy-start(bf16[32,5,24,128]{3,2,1,0:T(8,128)(2,1)S(1)} %all-to-all-done.1) | copy-start | bytes 2949124
  30.5 48.1 %all-to-all-start = ((bf16[32,8,24,256]{3,2,1,0:T(8,128)(2,1)}), bf16[32,8,24,256]{3,2,1,0:T(8,128)(2,1)}, u32[]{:S(2)}, u32[]{:S(2)}) async-start(bf16[32,8,24,256]{3,2,1,0:T(8,128)(2,1)} %pack_direct.1), calls=%async_computation | async-start | bytes 6291456 | tf_op jit(solution)/shard_map/all_to_all | solution.py:291
  37.4 25.1 %collective-permute-start.1 = (bf16[32,5,24,128]{3,2,1,0:T(8,128)(2,1)S(1)}, bf16[32,5,24,128]{3,2,1,0:T(8,128)(2,1)S(1)}, u32[]{:S(2)}, u32[]{:S(2)}) collective-permute-start(bf16[32,5,24,128]{3,2,1,0:T(8,128)(2,1)S(1)} %all-to-all-done.1), channel_id=1, source_target_pairs={{0,1},{1,2},{2,3},{3,0},{4,5},{5,6},{6,7},{7,4},{8,9},{9,10},{10,1... | collective-permute-start | bytes 2949128 | tf_op jit(solution)/shard_map/ppermute | solution.py:292
  39.0 24.9 %collective-permute-start = (bf16[32,5,24,128]{3,2,1,0:T(8,128)(2,1)S(1)}, bf16[32,5,24,128]{3,2,1,0:T(8,128)(2,1)S(1)}, u32[]{:S(2)}, u32[]{:S(2)}) collective-permute-start(bf16[32,5,24,128]{3,2,1,0:T(8,128)(2,1)S(1)} %all-to-all-done.1), channel_id=1, source_target_pairs={{0,3},{1,0},{2,1},{3,2},{4,7},{5,4},{6,5},{7,6},{8,11},{9,8},{10,9... | collective-permute-start | bytes 2949128 | tf_op jit(solution)/shard_map/ppermute | solution.py:293
  40.8 26.2 %copy-start.7 = (s32[20]{0:T(128)}, s32[20]{0:T(128)S(1)}, u32[]{:S(2)}) copy-start(s32[20]{0:T(128)S(1)} %and_select_fusion.8) | copy-start | bytes 244
  62.5 1.0 copy-start.5
  63.5 15.0 %collective-permute-start.2 = (bf16[16,5,24,128]{3,2,1,0:T(8,128)(2,1)S(1)}, bf16[16,5,24,128]{3,2,1,0:T(8,128)(2,1)S(1)}, u32[]{:S(2)}, u32[]{:S(2)}) collective-permute-start(bf16[16,5,24,128]{3,2,1,0:T(8,128)(2,1)S(1)} %slice.42), channel_id=1, source_target_pairs={{0,1},{1,2},{2,3},{3,0},{4,5},{5,6},{6,7},{7,4},{8,9},{9,10},{10,1... | collective-permute-start | bytes 1474568 | tf_op jit(solution)/shard_map/ppermute | solution.py:295
  63.9 3.1 %copy-start = (bf16[32,5,24,128]{3,2,1,0:T(8,128)(2,1)}, bf16[32,5,24,128]{3,2,1,0:T(8,128)(2,1)S(1)}, u32[]{:S(2)}) copy-start(bf16[32,5,24,128]{3,2,1,0:T(8,128)(2,1)S(1)} %collective-permute-done) | copy-start | bytes 2949124
  63.9 14.6 %collective-permute-start.3 = (bf16[16,5,24,128]{3,2,1,0:T(8,128)(2,1)S(1)}, bf16[16,5,24,128]{3,2,1,0:T(8,128)(2,1)S(1)}, u32[]{:S(2)}, u32[]{:S(2)}) collective-permute-start(bf16[16,5,24,128]{3,2,1,0:T(8,128)(2,1)S(1)} %slice.43), channel_id=1, source_target_pairs={{0,3},{1,0},{2,1},{3,2},{4,7},{5,4},{6,5},{7,6},{8,11},{9,8},{10,9... | collective-permute-start | bytes 1474568 | tf_op jit(solution)/shard_map/ppermute | solution.py:296
  67.0 11.6 %copy-start.2 = (s32[2]{0:T(128)S(1)}, s32[2]{0:T(128)}, u32[]{:S(2)}) copy-start(s32[2]{0:T(128)} %pad_add_fusion.core_ref) | copy-start | bytes 28
  67.0 11.6 %copy-start.3 = (s32[32]{0:T(128)S(1)}, s32[32]{0:T(128)}, u32[]{:S(2)}) copy-start(s32[32]{0:T(128)} %pad_add_fusion.1.places_ref) | copy-start | bytes 388
  78.6 1.2 copy-start.1
  96.7 2.5 %collective-permute-start.4 = (f32[1,4,24,2048]{3,2,1,0:T(8,128)S(1)}, f32[1,4,24,2048]{3,2,1,0:T(8,128)S(1)}, u32[]{:S(2)}, u32[]{:S(2)}) collective-permute-start(f32[1,4,24,2048]{3,2,1,0:T(8,128)S(1)} %bitcast.71), channel_id=1, source_target_pairs={{0,4},{4,0},{8,12},{12,8},{16,20},{20,16},{24,28},{28,24},{32,36},... | collective-permute-start | bytes 2359304 | tf_op jit(solution)/shard_map/ppermute | solution.py:275
  99.4 3.7 %collective-permute-start.7 = (f32[2,4,24,2048]{3,2,1,0:T(8,128)S(1)}, f32[2,4,24,2048]{3,2,1,0:T(8,128)S(1)}, u32[]{:S(2)}, u32[]{:S(2)}) collective-permute-start(f32[2,4,24,2048]{3,2,1,0:T(8,128)S(1)} %bitcast.69), channel_id=1, source_target_pairs={{0,4},{4,0},{8,12},{12,8},{16,20},{20,16},{24,28},{28,24},{32,36},... | collective-permute-start | bytes 4718600 | tf_op jit(solution)/shard_map/ppermute | solution.py:275
  99.6 7.1 %collective-permute-start.5 = (f32[1,4,24,2048]{3,2,1,0:T(8,128)S(1)}, f32[1,4,24,2048]{3,2,1,0:T(8,128)S(1)}, u32[]{:S(2)}, u32[]{:S(2)}) collective-permute-start(f32[1,4,24,2048]{3,2,1,0:T(8,128)S(1)} %bitcast.70), channel_id=1, source_target_pairs={{0,4},{4,0},{8,12},{12,8},{16,20},{20,16},{24,28},{28,24},{32,36},... | collective-permute-start | bytes 2359304 | tf_op jit(solution)/shard_map/ppermute | solution.py:275
  100.0 13.6 %collective-permute-start.6 = (f32[4,24,2048]{2,1,0:T(8,128)S(1)}, f32[4,24,2048]{2,1,0:T(8,128)S(1)}, u32[]{:S(2)}, u32[]{:S(2)}) collective-permute-start(f32[4,24,2048]{2,1,0:T(8,128)S(1)} %fusion.2), channel_id=1, source_target_pairs={{0,16},{4,68},{8,24},{12,76},{16,0},{20,84},{24,8},{28,92},{32,48}... | collective-permute-start | bytes 2359304 | tf_op jit(solution)/shard_map/ppermute | solution.py:271
  103.4 18.5 %collective-permute-start.8 = (f32[4,24,2048]{2,1,0:T(8,128)S(1)}, f32[4,24,2048]{2,1,0:T(8,128)S(1)}, u32[]{:S(2)}, u32[]{:S(2)}) collective-permute-start(f32[4,24,2048]{2,1,0:T(8,128)S(1)} %get-tuple-element.34), channel_id=1, source_target_pairs={{0,8},{4,36},{8,16},{12,44},{16,24},{20,52},{24,0},{28,60},{32,40}... | collective-permute-start | bytes 2359304 | tf_op jit(solution)/shard_map/ppermute | solution.py:271
  104.9 17.2 %collective-permute-start.9 = (f32[4,24,2048]{2,1,0:T(8,128)S(1)}, f32[4,24,2048]{2,1,0:T(8,128)S(1)}, u32[]{:S(2)}, u32[]{:S(2)}) collective-permute-start(f32[4,24,2048]{2,1,0:T(8,128)S(1)} %get-tuple-element.35), channel_id=1, source_target_pairs={{0,24},{4,100},{8,0},{12,108},{16,8},{20,116},{24,16},{28,124},{32... | collective-permute-start | bytes 2359304 | tf_op jit(solution)/shard_map/ppermute | solution.py:271
  122.4 7.3 %collective-permute-start.10 = (f32[24,2048]{1,0:T(8,128)S(1)}, f32[24,2048]{1,0:T(8,128)S(1)}, u32[]{:S(2)}, u32[]{:S(2)}) collective-permute-start(f32[24,2048]{1,0:T(8,128)S(1)} %get-tuple-element.36), channel_id=1, source_target_pairs={{0,64},{4,20},{8,72},{12,28},{16,80},{20,4},{24,88},{28,12},{32,96... | collective-permute-start | bytes 589832 | tf_op jit(solution)/shard_map/ppermute | solution.py:271
  125.6 6.4 %collective-permute-start.12 = (f32[24,2048]{1,0:T(8,128)S(1)}, f32[24,2048]{1,0:T(8,128)S(1)}, u32[]{:S(2)}, u32[]{:S(2)}) collective-permute-start(f32[24,2048]{1,0:T(8,128)S(1)} %get-tuple-element.37), channel_id=1, source_target_pairs={{0,96},{4,28},{8,104},{12,4},{16,112},{20,12},{24,120},{28,20},{32... | collective-permute-start | bytes 589832 | tf_op jit(solution)/shard_map/ppermute | solution.py:271
  126.7 6.9 %collective-permute-start.11 = (f32[24,2048]{1,0:T(8,128)S(1)}, f32[24,2048]{1,0:T(8,128)S(1)}, u32[]{:S(2)}, u32[]{:S(2)}) collective-permute-start(f32[24,2048]{1,0:T(8,128)S(1)} %get-tuple-element.38), channel_id=1, source_target_pairs={{0,32},{4,12},{8,40},{12,20},{16,48},{20,28},{24,56},{28,4},{32,64... | collective-permute-start | bytes 589832 | tf_op jit(solution)/shard_map/ppermute | solution.py:271
